TPU v7x, 128 devices: a whole 4x4x4 slice. The times are simulated.
128 devices in a mesh: dp: 16 (over z, x), seq: 8 (over y, core).
Axes of the slice: x: 4, y: 4, z: 4, core: 2. Of those that a mesh axis runs over, the one named last changes fastest.
Arguments:
- tokens: bfloat16 [98304, 2048], P(('dp', 'seq')), may hold values from -6 to 6
- norm_gain: float32 [2048], replicated, may hold values from 0.5 to 1.5
- qkv_weight: bfloat16 [3, 2048, 1024], replicated, may hold values from -0.125 to 0.125
- beta_weight: bfloat16 [2048, 8], replicated, may hold values from -0.125 to 0.125
- beta_bias: float32 [8], replicated, may hold values from -7 to 1
- out_weight: bfloat16 [1024, 2048], replicated, may hold values from -0.1875 to 0.1875
- doc_lengths: int32 [16, 8], replicated, may hold values from 1 to 3840, 6144 in all within a row
- source_dp: int32 [16, 8, 16], replicated, may hold values from 0 to 15, as said below
- source_offset: int32 [16, 8, 16], replicated, may hold values from 0 to 720, as said below
Outputs:
- mixed: bfloat16 [98304, 2048], P(('dp', 'seq'))
Inputs may be any that keep to these rules, and one draw needn't show every extreme that they name: `source_dp`: for each seq index j, the slots of all owners take every piece of 48 rows of every arrival device (p, j) exactly once, and no owner takes two pieces from one arrival device. `source_offset`: A multiple of 48. `doc_lengths`: each row sums to 6144.
All inputs are finite; a program needn't handle non-finite values.
Results may differ from a plain program's by a relative error of at most 0.02.
Values may be sent and summed in bfloat16 or wider, within the bound.
A program may use at most 128 MiB of HBM per device.

v0:
```python
import jax
import jax.numpy as jnp
from jax import lax
from jax.sharding import PartitionSpec as P

BLOCK = 64


rms_epsilon = 1e-06


def carried_in(x, axis, combine, identity):
    peers, position = (lax.axis_size(axis), lax.axis_index(axis))
    everything = jax.tree.map(lambda part: lax.all_gather(part, axis), x)
    start = jax.tree.map(
        lambda part, zero: jnp.broadcast_to(jnp.asarray(zero, part.dtype), part.shape), x, identity
    )

    def step(k, before):
        reached = k < position
        new = combine(before, jax.tree.map(lambda part: part[k], everything))
        return jax.tree.map(lambda a, b: jnp.where(reached, a, b), new, before)

    return lax.fori_loop(0, peers, step, start)


def combine_states(earlier, following):
    return (earlier[0] * following[0], earlier[1] * following[0][:, None, :] + following[1])


def chain_states(decay_all, local_state):
    identity = (jnp.ones_like(decay_all), jnp.zeros_like(local_state))
    return carried_in((decay_all, local_state), "seq", combine_states, identity)


def block_scores(block_query, block_key, block_total):
    rows_block, head_count, head_size = block_query.shape
    sub_rows = 16
    sub_count = rows_block // sub_rows
    query_sub = block_query.reshape(sub_count, sub_rows, head_count, head_size)
    key_sub = block_key.reshape(sub_count, sub_rows, head_count, head_size)
    total_sub = block_total.reshape(sub_count, sub_rows, head_count, head_size)
    near_gap = jnp.minimum(total_sub[:, :, None] - total_sub[:, None, :], 0.0)
    near_scores = jnp.sum(query_sub[:, :, None] * key_sub[:, None, :] * jnp.exp(near_gap), axis=-1)
    anchor = total_sub[:, -1]
    key_scaled = key_sub * jnp.exp(anchor[:, None] - total_sub)
    query_scaled = block_query[None] * jnp.exp(
        jnp.minimum(block_total[None] - anchor[:, None], 0.0)
    )
    far_scores = jnp.einsum(
        "btgc,bsgc->tbsg", query_scaled, key_scaled, precision=lax.Precision.HIGHEST
    ).reshape(rows_block, rows_block, head_count)
    same_sub = jnp.eye(sub_count, dtype=jnp.float32)
    near_full = (near_scores[:, :, None, :, :] * same_sub[:, None, :, None, None]).reshape(
        rows_block, rows_block, head_count
    )
    sub_of = jnp.arange(rows_block) // sub_rows
    inside = (sub_of[:, None] == sub_of[None, :])[:, :, None]
    return jnp.where(inside, near_full, far_scores)


def run_blocks(
    start_state,
    query_float,
    key_float,
    value_float,
    step_size,
    log_decay,
    log_total,
    doc_index,
    doc_start,
):
    tok_dev = query_float.shape[0]
    block_count = tok_dev // BLOCK

    def shaped(source_array):
        return source_array.reshape((block_count, BLOCK) + source_array.shape[1:])

    causal = jnp.arange(BLOCK)[:, None] >= jnp.arange(BLOCK)[None, :]

    def advance(state_now, inputs):
        (
            block_query,
            block_key,
            block_value,
            block_step,
            block_decay,
            block_total,
            block_doc,
            block_start,
        ) = inputs
        root = block_total[0] - block_decay[0]
        no_reset = (jnp.cumsum(block_start) == 0).astype(jnp.float32)
        same_doc = (block_doc[:, None] == block_doc[None, :]) & causal
        scores = block_scores(block_query, block_key, block_total)
        weights_ts = jnp.where(same_doc[:, :, None], scores, 0.0) * block_step[None, :, :]
        block_out = jnp.einsum("tsh,shi->thi", weights_ts, block_value)
        carried = jnp.exp(block_total - root) * no_reset[:, None, None]
        block_out = block_out + jnp.einsum("hij,thj->thi", state_now, block_query * carried)
        last_gap = jnp.exp(block_total[-1][None] - block_total)
        tail_weight = (block_doc == block_doc[-1]).astype(jnp.float32)[:, None] * block_step
        state_next = state_now * carried[-1][:, None, :]
        state_next = state_next + jnp.einsum(
            "shi,shj->hij", block_value * tail_weight[:, :, None], block_key * last_gap
        )
        return (state_next, block_out)

    series = (
        shaped(query_float),
        shaped(key_float),
        shaped(value_float),
        shaped(step_size),
        shaped(log_decay),
        shaped(log_total),
        shaped(doc_index),
        shaped(doc_start),
    )
    final_state, outputs = lax.scan(advance, start_state, series)
    return (final_state, outputs.reshape(query_float.shape))


def shards(
    tokens,
    norm_gain,
    qkv_weight,
    beta_weight,
    beta_bias,
    out_weight,
    doc_lengths,
    source_dp,
    source_offset,
):
    groups = lax.axis_size("dp")
    dp_index = lax.axis_index("dp")
    seq_index = lax.axis_index("seq")
    tok_dev, model_width = tokens.shape
    piece_rows = tok_dev // groups
    head_count = beta_weight.shape[1]
    head_size = qkv_weight.shape[2] // head_count
    plan_source = lax.dynamic_index_in_dim(source_dp, seq_index, 1, keepdims=False)
    plan_offset = lax.dynamic_index_in_dim(source_offset, seq_index, 1, keepdims=False)
    from_here = plan_source == dp_index
    sent_piece = jnp.sum(jnp.where(from_here, plan_offset, 0), axis=1) // piece_rows
    outgoing = tokens.reshape(groups, piece_rows, model_width)[sent_piece]
    incoming = lax.all_to_all(outgoing, "dp", split_axis=0, concat_axis=0, tiled=True)
    slot_source = lax.dynamic_index_in_dim(plan_source, dp_index, 0, keepdims=False)
    owned = incoming[slot_source].reshape(tok_dev, model_width)
    rows_float = owned.astype(jnp.float32)
    normed = (
        rows_float
        * lax.rsqrt(jnp.mean(rows_float * rows_float, axis=1, keepdims=True) + rms_epsilon)
        * norm_gain
    ).astype(jnp.bfloat16)
    query_rows = jnp.dot(normed, qkv_weight[0], preferred_element_type=jnp.float32).astype(
        jnp.bfloat16
    )
    key_rows = jnp.dot(normed, qkv_weight[1], preferred_element_type=jnp.float32).astype(
        jnp.bfloat16
    )
    value_rows = jnp.dot(normed, qkv_weight[2], preferred_element_type=jnp.float32).astype(
        jnp.bfloat16
    )
    strength = jax.nn.sigmoid(
        jnp.dot(normed, beta_weight, preferred_element_type=jnp.float32) + beta_bias
    )
    query_float = query_rows.astype(jnp.float32).reshape(tok_dev, head_count, head_size)
    key_float = key_rows.astype(jnp.float32).reshape(tok_dev, head_count, head_size)
    value_float = value_rows.astype(jnp.float32).reshape(tok_dev, head_count, head_size)
    step_size = strength / (1.0 + strength * jnp.sum(key_float * key_float, axis=2))
    log_decay = jnp.log(1.0 - step_size[:, :, None] * key_float * key_float)
    log_total = jnp.cumsum(log_decay, axis=0)
    lengths = lax.dynamic_index_in_dim(doc_lengths, dp_index, 0, keepdims=False)
    starts = jnp.cumsum(lengths) - lengths
    position = seq_index * tok_dev + jnp.arange(tok_dev, dtype=jnp.int32)
    doc_start = jnp.any(position[:, None] == starts[None, :], axis=1).astype(jnp.int32)
    doc_index = jnp.sum((starts[None, :] <= position[:, None]).astype(jnp.int32), axis=1)
    untouched = (jnp.cumsum(doc_start) == 0).astype(jnp.float32)
    decay_all = untouched[-1] * jnp.exp(log_total[-1])
    tail_weight = (doc_index == doc_index[-1]).astype(jnp.float32)[:, None] * step_size
    local_state = jnp.einsum(
        "shi,shj->hij",
        value_float * tail_weight[:, :, None],
        key_float * jnp.exp(log_total[-1][None] - log_total),
    )
    incoming_state = chain_states(decay_all, local_state)
    final_state, heads_out = run_blocks(
        incoming_state[1],
        query_float,
        key_float,
        value_float,
        step_size,
        log_decay,
        log_total,
        doc_index,
        doc_start,
    )
    attended = heads_out.reshape(tok_dev, head_count * head_size).astype(jnp.bfloat16)
    numbers = jnp.arange(groups, dtype=jnp.int32)
    slot_for = jnp.sum(
        jnp.where(slot_source[None, :] == numbers[:, None], numbers[None, :], 0), axis=1
    )
    target_for = jnp.sum(
        jnp.where(sent_piece[None, :] == numbers[:, None], numbers[None, :], 0), axis=1
    )
    projected = jnp.dot(attended, out_weight, preferred_element_type=jnp.float32).astype(
        jnp.bfloat16
    )
    returned = lax.all_to_all(
        projected.reshape(groups, piece_rows, model_width)[slot_for],
        "dp",
        split_axis=0,
        concat_axis=0,
        tiled=True,
    )
    return returned[target_for].reshape(tok_dev, model_width)


def solution(mesh):
    return jax.shard_map(
        shards,
        mesh=mesh,
        in_specs=(P(("dp", "seq"), None), P(), P(), P(), P(), P(), P(), P(), P()),
        out_specs=P(("dp", "seq"), None),
        check_vma=False,
    )
```

profile of v0, /device:TPU:24, one launch (start us, length us, event | category | flops | bytes accessed | tf_op | source)
XLA Modules:
  0.0 381.3 jit_solution(10046067165259979945)
XLA Ops:
  9.9 2.4 gather_fusion
  12.3 8.1 %all-to-all-start = ((bf16[16,48,2048]{2,1,0:T(8,128)(2,1)}), bf16[16,48,2048]{2,1,0:T(8,128)(2,1)}, u32[]{:S(2)}, u32[]{:S(2)}) async-start(bf16[16,48,2048]{2,1,0:T(8,128)(2,1)} %gather_fusion), calls=%async_computation | async-start | bytes 6291456 | tf_op jit(solution)/shard_map/all_to_all | solution.py:145
  25.4 42.6 %all-to-all-done = bf16[16,48,2048]{2,1,0:T(8,128)(2,1)} async-done(((bf16[16,48,2048]{2,1,0:T(8,128)(2,1)}), bf16[16,48,2048]{2,1,0:T(8,128)(2,1)}, u32[]{:S(2)}, u32[]{:S(2)}) %all-to-all-start) | async-done | bytes 3145760 | tf_op jit(solution)/shard_map/all_to_all | solution.py:145
  67.9 2.6 gather_fusion.1
  73.0 6.4 %convert_bitcast_fusion.1 = f32[96,8,8,128]{3,1,2,0:T(8,128)S(1)} fusion(bf16[768,2048]{1,0:T(8,128)(2,1)S(1)} %bitcast.244, bf16[3,2048,1024]{2,1,0:T(8,128)(2,1)} %param.15), kind=kOutput, calls=%fused_computation.93 | convolution fusion | flops 3222798336 | bytes 10485760 | tf_op jit(solution)/shard_map/dot_general | solution.py:157
  79.4 7.4 %fusion.55 = f32[768,1024]{1,0:T(8,128)} fusion(bf16[768,2048]{1,0:T(8,128)(2,1)S(1)} %bitcast.245, bf16[3,2048,1024]{2,1,0:T(8,128)(2,1)} %param.15), kind=kOutput, calls=%fused_computation.96 | convolution fusion | flops 3222798336 | bytes 10485760 | tf_op jit(solution)/shard_map/dot_general | solution.py:160
  89.2 2.7 fusion.28
  96.5 1.9 broadcast_add_fusion
  98.4 3.6 copy.134
  102.0 3.6 copy.135
  106.3 3.9 %exponential_multiply_fusion.2 = bf16[768,8,128]{2,1,0:T(8,128)(2,1)} fusion(f32[8,128]{1,0:T(8,128)S(1)} %get-tuple-element.413, f32[96,8,8,128]{3,2,1,0:T(8,128)S(1)} %copy.147, f32[128,8,768]{0,1,2:T(8,128)} %copy.135), kind=kLoop, calls=%fused_computation.90 | loop fusion | flops 2359296 | bytes 7868416 | tf_op jit(solution)/shard_map/mul | solution.py:183
  110.2 2.4 copy.144
  112.7 2.9 fusion.44
  116.0 4.5 %copy.149 = f32[96,8,8,128]{3,2,1,0:T(8,128)} copy(f32[96,8,8,128]{3,1,2,0:T(8,128)} %bitcast.238) | data formatting | bytes 6291456
  120.5 5.2 %convert_bitcast_fusion = f32[96,8,8,128]{3,1,2,0:T(8,128)S(1)} fusion(bf16[768,2048]{1,0:T(8,128)(2,1)S(1)} %bitcast.246, bf16[3,2048,1024]{2,1,0:T(8,128)(2,1)} %param.15), kind=kOutput, calls=%fused_computation.89 | convolution fusion | flops 3222798336 | bytes 10485760 | tf_op jit(solution)/shard_map/dot_general | solution.py:154
  125.7 2.5 copy.150
  128.2 12.8 %all_gather.10 = f32[8,8,128]{2,1,0:T(8,128)S(1)} all-gather(f32[1,8,128]{2,1,0:T(8,128)S(1)} %get-tuple-element.414), channel_id=1, replica_groups=mesh['dp'=16,'seq'=8] {'seq'}, dimensions={0}, use_global_device_ids=true | all-gather | bytes 36864 | tf_op jit(solution)/shard_map/all_gather | solution.py:14
  141.0 2.2 fusion.41
  144.7 12.2 %while.30 = (s32[]{:T(128)}, f32[8,128,128]{2,1,0:T(8,128)S(1)}, s32[]{:T(128)}, f32[8,8,128]{2,1,0:T(8,128)S(1)}, f32[8,8,128,128]{3,2,1,0:T(8,128)}, /*index=5*/s32[]{:T(128)}, s32[]{:T(128)}) while((s32[]{:T(128)}, f32[8,128,128]{2,1,0:T(8,128)S(1)}, s32[]{:T(128)}, f32[8,8,128]{2,1,0:T(8,128)S(1)}, ...), condition=%wide.region_11.12_spmd.clone, body=%wide.region_10.11_spmd.clone.sunk | while | flops 524292 | bytes 1585257 | solution.py:24
  157.0 146.4 %while.29 = (s32[]{:T(128)}, f32[8,128,128]{2,1,0:T(8,128)S(1)}, bf16[12,64,8,128]{3,1,2,0:T(8,128)(2,1)}, f32[12,64,8,128]{3,2,1,0:T(8,128)}, f32[12,64,8,128]{...) while((s32[]{:T(128)}, f32[8,128,128]{2,1,0:T(8,128)S(1)}, ...), condition=%wide.region_15.16_spmd.clone, body=%wide.region_12.15_spmd.clone.sunk | while | flops 99465440 | bytes 10957885 | solution.py:118
  174.8 1.8 convolution_bitcast_fusion.5
  187.0 1.8 convolution_bitcast_fusion.5
  199.2 1.8 convolution_bitcast_fusion.5
  223.6 1.8 convolution_bitcast_fusion.5
  235.8 1.8 convolution_bitcast_fusion.5
  272.4 1.8 convolution_bitcast_fusion.5
  303.4 2.6 copy.141
  306.0 5.8 %convolution_convert_fusion = bf16[768,2048]{1,0:T(8,128)(2,1)S(1)} fusion(bf16[1024,2048]{1,0:T(8,128)(2,1)} %param.18, bf16[96,8,8,128]{3,2,1,0:T(8,128)(2,1)S(1)} %bitcast.249), kind=kOutput, calls=%fused_computation.80 | convolution fusion | flops 3222798336 | bytes 8912896 | tf_op jit(solution)/shard_map/dot_general | solution.py:205
  311.9 2.4 gather_fusion.2
  314.3 7.1 %all-to-all-start.1 = ((bf16[16,48,2048]{2,1,0:T(8,128)(2,1)}), bf16[16,48,2048]{2,1,0:T(8,128)(2,1)}, u32[]{:S(2)}, u32[]{:S(2)}) async-start(bf16[16,48,2048]{2,1,0:T(8,128)(2,1)} %gather_fusion.2), calls=%async_computation.1 | async-start | bytes 6291456 | tf_op jit(solution)/shard_map/all_to_all | solution.py:208
  321.6 48.6 %all-to-all-done.1 = bf16[16,48,2048]{2,1,0:T(8,128)(2,1)} async-done(((bf16[16,48,2048]{2,1,0:T(8,128)(2,1)}), bf16[16,48,2048]{2,1,0:T(8,128)(2,1)}, u32[]{:S(2)}, u32[]{:S(2)}) %all-to-all-start.1) | async-done | bytes 3145760 | tf_op jit(solution)/shard_map/all_to_all | solution.py:208
  370.1 4.3 %gather_fusion.3 = bf16[16,48,2048]{2,1,0:T(8,128)(2,1)} fusion(bf16[16,48,2048]{2,1,0:T(8,128)(2,1)} %all-to-all-done.1, s32[1024]{0:T(1024)S(1)} %pad_clamp_fusion), kind=kCustom, calls=%fused_computation.3 | custom fusion | bytes 6291520 | tf_op jit(solution)/shard_map/gather | solution.py:215
  (502 shorter events, 165.7 us)
Async XLA Ops:
  6.5 3.3 copy-start
  12.3 8.1 %copy-start.13 = (s32[16,8]{0,1:T(8,128)S(1)}, s32[16,8]{0,1:T(8,128)}, u32[]{:S(2)}) copy-start(s32[16,8]{0,1:T(8,128)} %param.19) | copy-start | bytes 1540
  12.3 55.6 %all-to-all-start = ((bf16[16,48,2048]{2,1,0:T(8,128)(2,1)}), bf16[16,48,2048]{2,1,0:T(8,128)(2,1)}, u32[]{:S(2)}, u32[]{:S(2)}) async-start(bf16[16,48,2048]{2,1,0:T(8,128)(2,1)} %gather_fusion), calls=%async_computation | async-start | bytes 6291456 | tf_op jit(solution)/shard_map/all_to_all | solution.py:145
  20.4 124.4 %all-gather.3.cloned.1.call-start = ((), (), s32[]{:S(2)}) async-start(), calls=%async_computation.2 | async-start | bytes 4718592 | tf_op jit(solution)/shard_map/all_gather | solution.py:14
  70.6 2.4 copy-start.4
  70.6 1.6 copy-start.11
  73.0 6.4 %copy-start.5 = (bf16[16,48,2048]{2,1,0:T(8,128)(2,1)}, bf16[16,48,2048]{2,1,0:T(8,128)(2,1)S(1)}, u32[]{:S(2)}) copy-start(bf16[16,48,2048]{2,1,0:T(8,128)(2,1)S(1)} %multiply_convert_fusion) | copy-start | bytes 9437188
  87.5 18.8 %copy-start.2 = (f32[96,8,8,128]{3,2,1,0:T(8,128)}, f32[96,8,8,128]{3,2,1,0:T(8,128)S(1)}, u32[]{:S(2)}) copy-start(f32[96,8,8,128]{3,2,1,0:T(8,128)S(1)} %copy.147) | copy-start | bytes 9437188
  89.1 2.7 copy-start.9
  89.2 2.7 copy-start.10
  89.2 2.7 copy-start.14
  110.2 2.4 copy-start.8
  112.6 3.1 copy-start.12
  112.6 3.1 copy-start.15
  112.6 3.1 copy-start.7
  116.0 4.5 %copy-start.6 = (bf16[16,48,2048]{2,1,0:T(8,128)(2,1)S(1)}, bf16[16,48,2048]{2,1,0:T(8,128)(2,1)}, u32[]{:S(2)}) copy-start(bf16[16,48,2048]{2,1,0:T(8,128)(2,1)} %copy-done.5) | copy-start | bytes 9437188
  125.7 15.3 %copy-start.3 = (f32[96,8,8,128]{3,2,1,0:T(8,128)S(1)}, f32[96,8,8,128]{3,2,1,0:T(8,128)}, u32[]{:S(2)}) copy-start(f32[96,8,8,128]{3,2,1,0:T(8,128)} %copy-done.2) | copy-start | bytes 9437188
  314.3 7.1 %copy-start.16 = (s32[16]{0:T(128)S(1)}, s32[16]{0:T(128)}, u32[]{:S(2)}) copy-start(s32[16]{0:T(128)} %get-tuple-element.407) | copy-start | bytes 196
  314.3 55.8 %all-to-all-start.1 = ((bf16[16,48,2048]{2,1,0:T(8,128)(2,1)}), bf16[16,48,2048]{2,1,0:T(8,128)(2,1)}, u32[]{:S(2)}, u32[]{:S(2)}) async-start(bf16[16,48,2048]{2,1,0:T(8,128)(2,1)} %gather_fusion.2), calls=%async_computation.1 | async-start | bytes 6291456 | tf_op jit(solution)/shard_map/all_to_all | solution.py:208
  321.6 52.9 %copy-start.1 = (bf16[768,2048]{1,0:T(8,128)(2,1)S(1)}, bf16[768,2048]{1,0:T(8,128)(2,1)}, u32[]{:S(2)}) copy-start(bf16[768,2048]{1,0:T(8,128)(2,1)} %param.13) | copy-start | bytes 9437188
Sparse Core Ops, SparseCore 0:
  115.7 28.9 all-gather.2
where the time goes:
time: 386 us; the launch traced here: 381 us
  other arithmetic  97.1 us (25%)
  waiting for transfers between devices  92.6 us (24%)
  local copies, waits for them, and re-layouts  75.6 us (20%)
  matrix products  71.4 us (18%)
  starting transfers between devices  15.2 us (4%)
  between operations  14.4 us (4%)
  blocking collectives  12.8 us (3%)
    all_to_all x1, waiting for transfers between devices, shards(): lax.all_to_all(projected.reshape(groups, piece_rows, model_width)[slot_fo...  48.6 us
    all_to_all x1, waiting for transfers between devices, shards(): lax.all_to_all(outgoing, 'dp', split_axis=0, concat_axis=0, tiled=True)  42.6 us
    dot_general x12, matrix products, block_scores(): jnp.einsum('btgc,bsgc->tbsg', query_scaled, key_scaled, precision=lax.Pre...  21.1 us
    reduce_sum x12, other arithmetic, block_scores(): jnp.sum(query_sub[:, :, None] * key_sub[:, None, :] * jnp.exp(near_gap),...  14.9 us
    mul x12, other arithmetic, advance(): block_query * carried  14.1 us
    all_gather x1, blocking collectives, carried_in(): everything = jax.tree.map(lambda part: lax.all_gather(part, axis), x)  12.8 us
    mul x12, other arithmetic, advance(): block_key * last_gap  12.1 us
    select_n x8, other arithmetic, step(): return jax.tree.map(lambda a, b: jnp.where(reached, a, b), new, before)  12 us
  transfers between devices with their start and end apart: 3, of which 3 were waited for; matrix products, arithmetic and copies ran while one was open for 5% of the time, Pallas kernels for 0%

commit v1 on v0

v1 whole, which is shorter than its diff:
```python
import jax
import jax.numpy as jnp
import numpy as np
from jax import lax
from jax.experimental import pallas as pl
from jax.experimental.pallas import tpu as pltpu
from jax.sharding import PartitionSpec as P

PIECE = 48
SUB = 12


def decay_sums():
    row = np.arange(PIECE)[:, None]
    col = np.arange(PIECE)[None, :]

    def between(low, high):
        return ((col > low) & (col <= high)).astype(np.float32)

    mid = (row // SUB) * SUB + SUB // 2 - 1
    near = between(mid, row) - between(row, mid)
    half = (row // (2 * SUB)) * (2 * SUB) + SUB - 1
    pair = between(half, row) + between(row, half)
    middle = np.full_like(row, 2 * SUB - 1)
    whole = between(middle, row) + between(row, middle)
    before = between(np.full_like(row, -1), row)
    after = between(row, np.full_like(row, PIECE - 1))
    sums = np.concatenate([near, pair, whole, before, after], axis=0)
    return np.concatenate([sums, sums], axis=1)


def dot_nt(a, b):
    return lax.dot_general(a, b, (((1,), (1,)), ((), ())), preferred_element_type=jnp.float32)


def dot_tn(a, b):
    return lax.dot_general(a, b, (((0,), (0,)), ((), ())), preferred_element_type=jnp.float32)


def recurrence_kernel(
    slot_source, starts, place, q_ref, k_ref, v_ref, logit_ref, sums_ref,
    out_ref, carry_ref, state_ref, decay_ref, state, total,
):
    heads = state.shape[0]
    size = state.shape[1]
    state[...] = jnp.zeros_like(state)
    total[...] = jnp.ones_like(total)
    down = lax.broadcasted_iota(jnp.int32, (PIECE, PIECE), 0)
    across = lax.broadcasted_iota(jnp.int32, (PIECE, PIECE), 1)
    wide = lax.broadcasted_iota(jnp.int32, (PIECE, size), 0)
    causal = down >= across
    in_sub = causal & (down // SUB == across // SUB)
    in_pair = causal & (down // (2 * SUB) == across // (2 * SUB)) & (down // SUB != across // SUB)
    in_whole = causal & (down // (2 * SUB) != across // (2 * SUB))
    right_pair = (wide // SUB) % 2 == 1
    right_whole = wide >= 2 * SUB

    def document_of(position):
        count = jnp.zeros_like(position)
        for n in range(starts.shape[0]):
            count = count + (starts[n] <= position).astype(jnp.int32)
        return count

    @pl.loop(0, q_ref.shape[0])
    def _(slot):
        piece = slot_source[slot]
        first = place[0] + slot * PIECE
        doc_down = document_of(first + down)
        doc_across = document_of(first + across)
        doc_wide = document_of(first + wide)
        doc_before = document_of(first - 1)
        doc_last = document_of(first + PIECE - 1)
        same = doc_down == doc_across
        near_mask, pair_mask, whole_mask = in_sub & same, in_pair & same, in_whole & same
        reaches = (doc_wide == doc_before).astype(jnp.float32)
        stays = (doc_wide == doc_last).astype(jnp.float32)
        kept = (doc_last == doc_before).astype(jnp.float32)
        strength = 1.0 / (1.0 + jnp.exp(-logit_ref[piece]))
        rows = pl.ds(pl.multiple_of(slot * PIECE, PIECE), PIECE)
        for h in range(heads):
            cols = slice(h * size, (h + 1) * size)
            query = q_ref[piece, :, cols].astype(jnp.float32)
            key = k_ref[piece, :, cols].astype(jnp.float32)
            value = v_ref[piece, :, cols].astype(jnp.float32)
            squares = key * key
            now = strength[:, h : h + 1]
            step = now / (1.0 + now * jnp.sum(squares, axis=1, keepdims=True))
            log_decay = jnp.log(1.0 - step * squares)
            high = log_decay.astype(jnp.bfloat16)
            low = (log_decay - high.astype(jnp.float32)).astype(jnp.bfloat16)
            gaps = jnp.dot(
                sums_ref[...], jnp.concatenate([high, low], axis=0),
                preferred_element_type=jnp.float32,
            )
            near = gaps[:PIECE]
            pair = gaps[PIECE : 2 * PIECE]
            whole = gaps[2 * PIECE : 3 * PIECE]
            before = gaps[3 * PIECE : 4 * PIECE]
            after = gaps[4 * PIECE :]
            near_query = (query * jnp.exp(near)).astype(jnp.bfloat16)
            near_key = (key * jnp.exp(-near)).astype(jnp.bfloat16)
            pair_both = (jnp.where(right_pair, query, key) * jnp.exp(pair)).astype(jnp.bfloat16)
            whole_both = (jnp.where(right_whole, query, key) * jnp.exp(whole)).astype(jnp.bfloat16)
            scores = jnp.where(
                near_mask,
                dot_nt(near_query, near_key),
                jnp.where(
                    pair_mask,
                    dot_nt(pair_both, pair_both),
                    jnp.where(whole_mask, dot_nt(whole_both, whole_both), 0.0),
                ),
            )
            stepped = value * step
            carried = query * (jnp.exp(before) * reaches)
            now_state = state[h]
            out = jnp.dot(
                scores.astype(jnp.bfloat16), stepped.astype(jnp.bfloat16),
                preferred_element_type=jnp.float32,
            )
            out = out + dot_nt(carried.astype(jnp.bfloat16), now_state.astype(jnp.bfloat16))
            out_ref[rows, cols] = out
            total_now = total[h : h + 1, :]
            carry_ref[rows, cols] = (carried * total_now).astype(jnp.bfloat16)
            decay = jnp.exp(before[PIECE - 1 :, :]) * kept
            total[h : h + 1, :] = total_now * decay
            state[h] = now_state * decay + dot_tn(
                stepped.astype(jnp.bfloat16),
                (key * (jnp.exp(after) * stays)).astype(jnp.bfloat16),
            )

    state_ref[...] = state[...]
    decay_ref[...] = total[...]


def recurrence(slot_source, starts, place, q, k, v, logits):
    pieces, piece_rows, width = q.shape
    heads = logits.shape[2]
    size = width // heads
    sums = jnp.asarray(decay_sums(), jnp.bfloat16)
    smem = pl.BlockSpec(memory_space=pltpu.SMEM)
    vmem = pl.BlockSpec(memory_space=pltpu.VMEM)
    return pl.pallas_call(
        recurrence_kernel,
        out_shape=(
            jax.ShapeDtypeStruct((pieces * piece_rows, width), jnp.float32),
            jax.ShapeDtypeStruct((pieces * piece_rows, width), jnp.bfloat16),
            jax.ShapeDtypeStruct((heads, size, size), jnp.float32),
            jax.ShapeDtypeStruct((heads, size), jnp.float32),
        ),
        in_specs=[smem] * 3 + [vmem] * 5,
        out_specs=[vmem] * 4,
        scratch_shapes=[
            pltpu.VMEM((heads, size, size), jnp.float32),
            pltpu.VMEM((heads, size), jnp.float32),
        ],
        compiler_params=pltpu.CompilerParams(vmem_limit_bytes=40 << 20),
    )(slot_source, starts, place, q, k, v, logits, sums)


rms_epsilon = 1e-06


def shards(
    tokens,
    norm_gain,
    qkv_weight,
    beta_weight,
    beta_bias,
    out_weight,
    doc_lengths,
    source_dp,
    source_offset,
):
    groups = lax.axis_size("dp")
    dp_index = lax.axis_index("dp")
    seq_index = lax.axis_index("seq")
    tok_dev, model_width = tokens.shape
    piece_rows = tok_dev // groups
    head_count = beta_weight.shape[1]
    head_size = qkv_weight.shape[2] // head_count
    plan_source = lax.dynamic_index_in_dim(source_dp, seq_index, 1, keepdims=False)
    plan_offset = lax.dynamic_index_in_dim(source_offset, seq_index, 1, keepdims=False)
    from_here = plan_source == dp_index
    sent_piece = jnp.sum(jnp.where(from_here, plan_offset, 0), axis=1) // piece_rows
    outgoing = tokens.reshape(groups, piece_rows, model_width)[sent_piece]
    incoming = lax.all_to_all(outgoing, "dp", split_axis=0, concat_axis=0, tiled=True)
    slot_source = lax.dynamic_index_in_dim(plan_source, dp_index, 0, keepdims=False)
    owned = incoming.reshape(tok_dev, model_width)
    rows_float = owned.astype(jnp.float32)
    normed = (
        rows_float
        * lax.rsqrt(jnp.mean(rows_float * rows_float, axis=1, keepdims=True) + rms_epsilon)
        * norm_gain
    ).astype(jnp.bfloat16)
    query_rows, key_rows, value_rows = (
        jnp.dot(normed, qkv_weight[n], preferred_element_type=jnp.float32)
        .astype(jnp.bfloat16)
        .reshape(groups, piece_rows, -1)
        for n in range(3)
    )
    logits = jnp.dot(normed, beta_weight, preferred_element_type=jnp.float32) + beta_bias
    logits = logits.reshape(groups, piece_rows, head_count)
    lengths = lax.dynamic_index_in_dim(doc_lengths, dp_index, 0, keepdims=False)
    starts = jnp.cumsum(lengths) - lengths
    place = (seq_index * tok_dev).astype(jnp.int32).reshape(1)
    heads_out, carried, local_state, decay_all = recurrence(
        slot_source, starts, place, query_rows, key_rows, value_rows, logits
    )
    all_decay = lax.all_gather(decay_all, "seq")
    all_state = lax.all_gather(local_state, "seq")
    before = jnp.zeros_like(local_state)
    for k in range(lax.axis_size("seq") - 1):
        before = jnp.where(k < seq_index, before * all_decay[k][:, None, :] + all_state[k], before)
    heads_out = heads_out.reshape(tok_dev, head_count, head_size) + jnp.einsum(
        "thj,hij->thi",
        carried.reshape(tok_dev, head_count, head_size),
        before.astype(jnp.bfloat16),
        preferred_element_type=jnp.float32,
    )
    attended = heads_out.reshape(tok_dev, head_count * head_size).astype(jnp.bfloat16)
    numbers = jnp.arange(groups, dtype=jnp.int32)
    slot_for = jnp.sum(
        jnp.where(slot_source[None, :] == numbers[:, None], numbers[None, :], 0), axis=1
    )
    target_for = jnp.sum(
        jnp.where(sent_piece[None, :] == numbers[:, None], numbers[None, :], 0), axis=1
    )
    returned = lax.all_to_all(
        attended.reshape(groups, piece_rows, -1)[slot_for],
        "dp",
        split_axis=0,
        concat_axis=0,
        tiled=True,
    )
    returned = returned[target_for].reshape(tok_dev, -1)
    return jnp.dot(returned, out_weight, preferred_element_type=jnp.float32).astype(jnp.bfloat16)


def solution(mesh):
    return jax.shard_map(
        shards,
        mesh=mesh,
        in_specs=(P(("dp", "seq"), None), P(), P(), P(), P(), P(), P(), P(), P()),
        out_specs=P(("dp", "seq"), None),
        check_vma=False,
    )
```

time: 386 us -> 233 us (0.60)
  other arithmetic: 97.1 us -> 9.97 us
  local copies, waits for them, and re-layouts: 75.6 us -> 30.2 us
  matrix products: 71.4 us -> 30.8 us
  Pallas kernels: 0 us -> 33.5 us
  waiting for transfers between devices: 92.6 us -> 84.1 us
    dot_general x53 -> x5, matrix products: 69.8 us -> 29.3 us  [the longest x3 16 us: shards(): jnp.dot(normed, qkv_weight[n], preferred_element_type=jnp.float32)]
    pallas_call x0 -> x1, Pallas kernels: none -> 33.5 us  [recurrence(): pl.pallas_call(recurrence_kernel, out_shape=(jax.ShapeDtypeStruct((pieces...]
    mul x61 -> x0, other arithmetic: 32.4 us -> none  [the longest x12 14.1 us: advance(): block_query * carried]
    all_to_all x1, waiting for transfers between devices: 48.6 us -> 25.3 us  [shards(): lax.all_to_all(attended.reshape(groups, piece_rows, -1)[slot_for], 'dp',...]
    reduce_sum x14 -> x0, other arithmetic: 15.8 us -> none  [the longest x12 14.9 us: block_scores(): jnp.sum(query_sub[:, :, None] * key_sub[:, None, :] * jnp.exp(near_gap),...]
    select_n x23 -> x3, other arithmetic: 13.2 us -> 0.03 us  [the longest x1 0.01 us: shards(): outgoing = tokens.reshape(groups, piece_rows, model_width)[sent_piece]]
    dynamic_slice x36 -> x0, local copies, waits for them, and re-layouts: 11.9 us -> none  [run_blocks(): final_state, outputs = lax.scan(advance, start_state, series)]
    mul x80 -> x0, local copies, waits for them, and re-layouts: 11.7 us -> none  [the longest x48 11 us: block_scores(): near_scores[:, :, None, :, :] * same_sub[:, None, :, None, None]]
  transfers between devices with their start and end apart: 3 -> 3, of which waited for: 3 -> 3; matrix products, arithmetic and copies ran while one was open for 5% -> 2% of each run, Pallas kernels for 0% -> 0%
where the time goes in v1:
time: 233 us; the launch traced here: 230 us
  waiting for transfers between devices  84.1 us (36%)
  Pallas kernels  33.5 us (14%)
  matrix products  30.8 us (13%)
  local copies, waits for them, and re-layouts  30.2 us (13%)
  starting transfers between devices  15 us (6%)
  between operations  13.6 us (6%)
  blocking collectives  13 us (6%)
  other arithmetic  9.97 us (4%)
    all_to_all x1, waiting for transfers between devices, shards(): lax.all_to_all(outgoing, 'dp', split_axis=0, concat_axis=0, tiled=True)  46.4 us
    pallas_call x1, Pallas kernels, recurrence(): pl.pallas_call(recurrence_kernel, out_shape=(jax.ShapeDtypeStruct((pieces...  33.5 us
    all_to_all x1, waiting for transfers between devices, shards(): lax.all_to_all(attended.reshape(groups, piece_rows, -1)[slot_for], 'dp',...  25.3 us
    dot_general x3, matrix products, shards(): jnp.dot(normed, qkv_weight[n], preferred_element_type=jnp.float32)  16 us
    all_gather x1, blocking collectives, shards(): all_decay = lax.all_gather(decay_all, 'seq')  13 us
    all_gather x1, waiting for transfers between devices, shards(): all_state = lax.all_gather(local_state, 'seq')  12.4 us
    unnamed x30, local copies, waits for them, and re-layouts  9.34 us
    all_to_all x1, starting transfers between devices, shards(): lax.all_to_all(outgoing, 'dp', split_axis=0, concat_axis=0, tiled=True)  8.05 us
  transfers between devices with their start and end apart: 3, of which 3 were waited for; matrix products, arithmetic and copies ran while one was open for 2% of the time, Pallas kernels for 0%

profile of v1, /device:TPU:24, one launch (start us, length us, event | category | flops | bytes accessed | tf_op | source)
XLA Modules:
  0.0 230.2 jit_solution(7689808927279988627)
XLA Ops:
  6.5 1.4 fusion.47
  8.5 2.4 %gather_fusion = bf16[16,48,2048]{2,1,0:T(8,128)(2,1)} fusion(bf16[16,48,2048]{2,1,0:T(8,128)(2,1)S(1)} %bitcast.73, s32[1024]{0:T(1024)S(1)} %pad_clamp_fusion.2), kind=kCustom, calls=%fused_computation | custom fusion | bytes 6291520 | tf_op jit(solution)/shard_map/gather | solution.py:185
  10.9 8.1 %all-to-all-start = ((bf16[16,48,2048]{2,1,0:T(8,128)(2,1)}), bf16[16,48,2048]{2,1,0:T(8,128)(2,1)}, u32[]{:S(2)}, u32[]{:S(2)}) async-start(bf16[16,48,2048]{2,1,0:T(8,128)(2,1)} %gather_fusion), calls=%async_computation | async-start | bytes 6291456 | tf_op jit(solution)/shard_map/all_to_all | solution.py:186
  19.4 0.7 fusion.48.slot_source
  20.1 46.4 %all-to-all-done = bf16[16,48,2048]{2,1,0:T(8,128)(2,1)} async-done(((bf16[16,48,2048]{2,1,0:T(8,128)(2,1)}), bf16[16,48,2048]{2,1,0:T(8,128)(2,1)}, u32[]{:S(2)}, u32[]{:S(2)}) %all-to-all-start) | async-done | bytes 3145760 | tf_op jit(solution)/shard_map/all_to_all | solution.py:186
  66.5 2.6 %multiply_reduce_fusion = f32[16,48]{1,0:T(8,128)S(1)} fusion(bf16[16,48,2048]{2,1,0:T(8,128)(2,1)} %all-to-all-done), kind=kLoop, calls=%fused_computation.7 | loop fusion | flops 4717824 | bytes 3148800 | tf_op jit(solution)/shard_map/reduce_sum | solution.py:192
  69.2 2.8 %multiply_convert_fusion = bf16[16,48,2048]{2,1,0:T(8,128)(2,1)S(1)} fusion(f32[2048]{0:T(1024)S(1)} %copy-done.9, f32[16,48]{1,0:T(8,128)S(1)} %add_rsqrt_fusion, bf16[16,48,2048]{2,1,0:T(8,128)(2,1)} %all-to-all-done), kind=kLoop, calls=%fused_computation.6 | loop fusion | flops 6291456 | bytes 6302720 | tf_op jit(solution)/shard_map/convert_element_type | solution.py:194
  72.0 6.9 %fusion.15 = bf16[768,1024]{1,0:T(8,128)(2,1)} fusion(bf16[768,2048]{1,0:T(8,128)(2,1)S(1)} %bitcast.79, bf16[3,2048,1024]{2,1,0:T(8,128)(2,1)} %param.12), kind=kOutput, calls=%fused_computation.21 | convolution fusion | flops 3222011904 | bytes 8912896 | tf_op jit(solution)/shard_map/dot_general | solution.py:196
  79.0 4.6 %fusion.18 = bf16[768,1024]{1,0:T(8,128)(2,1)} fusion(bf16[768,2048]{1,0:T(8,128)(2,1)S(1)} %bitcast.80, bf16[3,2048,1024]{2,1,0:T(8,128)(2,1)S(1)} %bitcast.85), kind=kOutput, calls=%fused_computation.22 | convolution fusion | flops 3222011904 | bytes 8912896 | tf_op jit(solution)/shard_map/dot_general | solution.py:196
  83.6 4.5 %fusion.12 = bf16[768,1024]{1,0:T(8,128)(2,1)} fusion(bf16[768,2048]{1,0:T(8,128)(2,1)S(1)} %bitcast.81, bf16[3,2048,1024]{2,1,0:T(8,128)(2,1)S(1)} %bitcast.85), kind=kOutput, calls=%fused_computation.20 | convolution fusion | flops 3222011904 | bytes 8912896 | tf_op jit(solution)/shard_map/dot_general | solution.py:196
  88.1 2.7 %fusion.1 = bf16[768,2048]{1,0:T(8,128)(2,1)S(1)} fusion(f32[2048]{0:T(1024)S(1)} %copy-done.9, f32[768]{0:T(1024)S(1)} %rsqrt.13, bf16[16,48,2048]{2,1,0:T(8,128)(2,1)} %all-to-all-done), kind=kLoop, calls=%fused_computation.5 | loop fusion | flops 6291456 | bytes 6302720 | tf_op jit(solution)/shard_map/convert_element_type | solution.py:194
  90.8 1.5 convolution_add_fusion
  92.3 0.9 copy.22
  93.3 1.4 copy-done.2
  94.7 1.4 copy-done.3
  96.1 1.4 copy-done.4
  97.5 0.8 copy-done.6
  98.3 33.5 %shard_map.100 = (f32[768,1024]{1,0:T(8,128)S(1)}, bf16[768,1024]{1,0:T(8,128)(2,1)S(1)}, f32[8,128,128]{2,1,0:T(8,128)S(1)}, f32[8,128]{1,0:T(8,128)S(1)}) custom-call(s32[16]{0:T(128)S(1)} %fusion.48.slot_source, s32[8]{0:T(128)S(1)} %bitcast_subtract_fusion.starts, s32[1]{0:T(128)} %bitcast.2.place, bf16[16,48,1024]{2,1,0:T(8,128)(2,1)S(1)} %bitcast.77, ...), custom_call_target="tpu_custom_call" | custom-call | tf_op jit(solution)/shard_map/pallas_call | solution.py:142
  131.8 1.7 copy-done.1
  133.5 0.8 copy-done.5
  134.3 1.3 copy-done.7
  135.8 3.5 %copy.26 = f32[768,1024]{0,1:T(8,128)} copy(f32[768,1024]{1,0:T(8,128)} %copy-done.1) | data formatting | bytes 6291456 | tf_op jit(solution)/shard_map/reshape | solution.py:214
  139.3 13.0 %all-gather = f32[64,128]{1,0:T(8,128)S(1)} all-gather(f32[8,128]{1,0:T(8,128)S(1)} %get-tuple-element.10), channel_id=2, replica_groups=mesh['dp'=16,'seq'=8] {'seq'}, dimensions={0}, use_global_device_ids=true | all-gather | bytes 36864 | tf_op jit(solution)/shard_map/all_gather | solution.py:209
  152.3 12.4 %all-gather.4.cloned.1.call-done = f32[64,128,128]{2,1,0:T(8,128)} async-done(((f32[8,128,128]{2,1,0:T(8,128)}), f32[64,128,128]{2,1,0:T(8,128)}) %all-gather.4.cloned.1.call-update) | async-done | bytes 4194320 | tf_op jit(solution)/shard_map/all_gather | solution.py:210
  164.7 5.5 %fusion.11 = bf16[768,8,128]{0,2,1:T(8,128)(2,1)} fusion(f32[768,8,128]{0,2,1:T(8,128)} %bitcast.78, f32[64,128,128]{2,1,0:T(8,128)} %all-gather.4.cloned.1.call-done, f32[8,128]{1,0:T(8,128)S(1)} %get-tuple-element.20, f32[8,128]{1,0:T(8,128)S(1)} %get-tuple-element.21, f32[8,128]{1,0:T(8,128)S(1)} %get-tuple-element.16, ...), kind=kOutput, calls=%fused_computation.19 | convolution fusion | flops 205651968 | bytes 9990151 | tf_op jit(solution)/shard_map/thj,hij->thi/dot_general | solution.py:214
  170.2 2.9 %copy.25 = bf16[768,8,128]{2,1,0:T(8,128)(2,1)} copy(bf16[768,8,128]{0,2,1:T(8,128)(2,1)} %fusion.11) | data formatting | bytes 3145728 | tf_op jit(solution)/shard_map/convert_element_type | solution.py:220
  173.1 3.7 %convert_element_type.55 = bf16[16,48,1024]{2,1,0:T(8,128)(2,1)} reshape(bf16[768,8,128]{2,1,0:T(8,128)(2,1)} %copy.25) | data formatting | bytes 3145728 | tf_op jit(solution)/shard_map/convert_element_type | solution.py:220
  176.8 3.2 %gather_fusion.1 = bf16[16,48,1024]{2,1,0:T(8,128)(2,1)} fusion(bf16[16,48,1024]{2,1,0:T(8,128)(2,1)} %convert_element_type.55, s32[1024]{0:T(1024)S(1)} %pad_clamp_fusion.1), kind=kCustom, calls=%fused_computation.1 | custom fusion | bytes 3145792 | tf_op jit(solution)/shard_map/gather | solution.py:229
  180.0 6.9 %all-to-all-start.1 = ((bf16[16,48,1024]{2,1,0:T(8,128)(2,1)}), bf16[16,48,1024]{2,1,0:T(8,128)(2,1)}, u32[]{:S(2)}, u32[]{:S(2)}) async-start(bf16[16,48,1024]{2,1,0:T(8,128)(2,1)} %gather_fusion.1), calls=%async_computation.1 | async-start | bytes 3145728 | tf_op jit(solution)/shard_map/all_to_all | solution.py:228
  187.1 25.3 %all-to-all-done.1 = bf16[16,48,1024]{2,1,0:T(8,128)(2,1)} async-done(((bf16[16,48,1024]{2,1,0:T(8,128)(2,1)}), bf16[16,48,1024]{2,1,0:T(8,128)(2,1)}, u32[]{:S(2)}, u32[]{:S(2)}) %all-to-all-start.1) | async-done | bytes 1572896 | tf_op jit(solution)/shard_map/all_to_all | solution.py:228
  212.4 3.2 %gather_fusion.2 = bf16[16,48,1024]{2,1,0:T(8,128)(2,1)} fusion(bf16[16,48,1024]{2,1,0:T(8,128)(2,1)} %all-to-all-done.1, s32[1024]{0:T(1024)S(1)} %pad_clamp_fusion), kind=kCustom, calls=%fused_computation.2 | custom fusion | bytes 3145792 | tf_op jit(solution)/shard_map/gather | solution.py:235
  215.6 7.7 %convolution_convert_fusion = bf16[768,2048]{1,0:T(8,128)(2,1)} fusion(bf16[768,1024]{1,0:T(8,128)(2,1)} %bitcast.82, bf16[1024,2048]{1,0:T(8,128)(2,1)} %param.15), kind=kOutput, calls=%fused_computation.17 | convolution fusion | flops 3222798336 | bytes 8912896 | tf_op jit(solution)/shard_map/dot_general | solution.py:236
  (41 shorter events, 1.4 us)
Async XLA Ops:
  6.5 2.0 copy-start
  10.9 8.1 %copy-start.10 = (s32[16,8]{0,1:T(8,128)S(1)}, s32[16,8]{0,1:T(8,128)}, u32[]{:S(2)}) copy-start(s32[16,8]{0,1:T(8,128)} %param.16) | copy-start | bytes 1540
  10.9 55.6 %all-to-all-start = ((bf16[16,48,2048]{2,1,0:T(8,128)(2,1)}), bf16[16,48,2048]{2,1,0:T(8,128)(2,1)}, u32[]{:S(2)}, u32[]{:S(2)}) async-start(bf16[16,48,2048]{2,1,0:T(8,128)(2,1)} %gather_fusion), calls=%async_computation | async-start | bytes 6291456 | tf_op jit(solution)/shard_map/all_to_all | solution.py:186
  19.0 50.2 %copy-start.9 = (f32[2048]{0:T(1024)S(1)}, f32[2048]{0:T(1024)}, u32[]{:S(2)}) copy-start(f32[2048]{0:T(1024)} %param.11) | copy-start | bytes 24580
  19.0 145.7 %all-gather.4.cloned.1.call-start = ((), (), s32[]{:S(2)}) async-start(), calls=%async_computation.2 | async-start | bytes 4718592 | tf_op jit(solution)/shard_map/all_gather | solution.py:210
  69.2 9.8 %slice-start = ((s8[12582912]{0:T(1024)(128)(4,1)}), s8[4194304]{0:T(1024)(128)(4,1)S(1)}, s32[]{:S(2)}) async-start(s8[12582912]{0:T(1024)(128)(4,1)} %bitcast.84), calls=%async_computation.3 | async-start | bytes 8388608
  72.0 6.9 %slice-start.1 = ((s8[12582912]{0:T(1024)(128)(4,1)}), s8[4194304]{0:T(1024)(128)(4,1)S(1)}, s32[]{:S(2)}) async-start(s8[12582912]{0:T(1024)(128)(4,1)} %bitcast.84), calls=%async_computation.4 | async-start | bytes 8388608
  72.0 6.9 %slice-start.2 = ((s8[12582912]{0:T(1024)(128)(4,1)}), s8[4194304]{0:T(1024)(128)(4,1)S(1)}, s32[]{:S(2)}) async-start(s8[12582912]{0:T(1024)(128)(4,1)} %bitcast.84), calls=%async_computation.5 | async-start | bytes 8388608
  88.1 2.7 %copy-start.8 = (bf16[2048,8]{0,1:T(8,128)(2,1)S(1)}, bf16[2048,8]{0,1:T(8,128)(2,1)}, u32[]{:S(2)}) copy-start(bf16[2048,8]{0,1:T(8,128)(2,1)} %param.13) | copy-start | bytes 98308
  88.1 2.7 %copy-start.11 = (f32[8]{0:T(128)S(1)}, f32[8]{0:T(128)}, u32[]{:S(2)}) copy-start(f32[8]{0:T(128)} %param.14) | copy-start | bytes 100
  93.2 1.4 copy-start.2
  94.7 1.4 copy-start.3
  96.1 1.4 copy-start.4
  97.5 0.8 copy-start.6
  131.8 1.7 copy-start.1
  133.5 0.8 copy-start.5
  134.3 1.3 copy-start.7
  180.0 32.4 %all-to-all-start.1 = ((bf16[16,48,1024]{2,1,0:T(8,128)(2,1)}), bf16[16,48,1024]{2,1,0:T(8,128)(2,1)}, u32[]{:S(2)}, u32[]{:S(2)}) async-start(bf16[16,48,1024]{2,1,0:T(8,128)(2,1)} %gather_fusion.1), calls=%async_computation.1 | async-start | bytes 3145728 | tf_op jit(solution)/shard_map/all_to_all | solution.py:228
Sparse Core Ops, SparseCore 0:
  135.7 28.8 all-gather.3

commit v2 on v1

--- a/solution.py
+++ b/solution.py
@@ -5,6 +5,123 @@
 from jax.experimental import pallas as pl
 from jax.experimental.pallas import tpu as pltpu
 from jax.sharding import PartitionSpec as P
+
+MESH = pl.DeviceIdType.MESH
+rms_epsilon = 1e-06
+ORDER = [(1, 0), (3, 3), (2, 3), (1, 3), (1, 2), (0, 1), (2, 0), (3, 0), (3, 1), (2, 2), (0, 2), (3, 2), (1, 1), (0, 3), (2, 1)]
+
+
+def peer_along(offset, sign):
+    me = lax.axis_index("dp")
+    down, right = offset
+    row = lax.rem(me // 4 + (down if sign > 0 else 4 - down), 4)
+    column = lax.rem(lax.rem(me, 4) + (right if sign > 0 else 4 - right), 4)
+    return row * 4 + column
+
+
+def greet_group(barrier, groups):
+    me, seq = lax.axis_index("dp"), lax.axis_index("seq")
+    for distance in range(1, groups):
+        pl.semaphore_signal(
+            barrier, inc=1, device_id=(lax.rem(me + distance, groups), seq), device_id_type=MESH
+        )
+
+
+def arrive_kernel(
+    sent, tokens, gain_ref, weight, beta_ref, bias_ref, q_ref, k_ref, v_ref, logit_ref,
+    held, send, recv, weight_held, normed, token_sem, weight_sem, send_sem, recv_sem,
+):
+    groups, piece_rows, model_width = held.shape
+    width = q_ref.shape[2]
+    me, seq = lax.axis_index("dp"), lax.axis_index("seq")
+    token_copy = pltpu.make_async_copy(tokens, held, token_sem)
+    token_copy.start()
+    weight_copy = pltpu.make_async_copy(weight, weight_held, weight_sem)
+    barrier = pltpu.get_barrier_semaphore()
+    greet_group(barrier, groups)
+    token_copy.wait()
+    weight_copy.start()
+    recv[me] = held[sent[me]]
+    pl.semaphore_wait(barrier, groups - 1)
+    copies = []
+    for offset in ORDER:
+        target = peer_along(offset, 1)
+        send[target] = held[sent[target]]
+        copy = pltpu.make_async_remote_copy(
+            src_ref=send.at[target], dst_ref=recv.at[me], send_sem=send_sem.at[target],
+            recv_sem=recv_sem.at[me], device_id=(target, seq), device_id_type=MESH,
+        )
+        copy.start()
+        copies.append(copy)
+    weight_copy.wait()
+    sources = [me] + [peer_along(offset, -1) for offset in ORDER]
+    together = normed.shape[0] // piece_rows
+    for first in range(0, groups, together):
+        for n in range(together):
+            source = sources[first + n]
+            if first + n > 0:
+                pltpu.make_async_remote_copy(
+                    src_ref=send.at[source], dst_ref=recv.at[source], send_sem=send_sem.at[source],
+                    recv_sem=recv_sem.at[source], device_id=(source, seq), device_id_type=MESH,
+                ).wait_recv()
+            rows = recv[source].astype(jnp.float32)
+            normed[n * piece_rows : (n + 1) * piece_rows, :] = (
+                rows
+                * lax.rsqrt(jnp.mean(rows * rows, axis=1, keepdims=True) + rms_epsilon)
+                * gain_ref[...]
+            ).astype(jnp.bfloat16)
+        logits = (
+            jnp.dot(normed[...], beta_ref[...], preferred_element_type=jnp.float32) + bias_ref[...]
+        )
+        for n in range(together):
+            logit_ref[sources[first + n]] = logits[n * piece_rows : (n + 1) * piece_rows]
+        tile = 512
+        for part, target_ref in enumerate((q_ref, k_ref, v_ref)):
+            for start in range(0, width, tile):
+                cols = slice(start, start + tile)
+                product = jnp.dot(
+                    normed[...], weight_held[part, :, cols], preferred_element_type=jnp.float32
+                ).astype(jnp.bfloat16)
+                for n in range(together):
+                    target_ref[sources[first + n], :, cols] = product[
+                        n * piece_rows : (n + 1) * piece_rows
+                    ]
+    for copy in copies:
+        copy.wait_send()
+
+
+def arrive(sent, tokens, gain, weight, beta, bias):
+    groups = sent.shape[0]
+    rows, model_width = tokens.shape
+    piece_rows = rows // groups
+    width = weight.shape[2]
+    heads = beta.shape[1]
+    smem = pl.BlockSpec(memory_space=pltpu.SMEM)
+    vmem = pl.BlockSpec(memory_space=pltpu.VMEM)
+    hbm = pl.BlockSpec(memory_space=pl.ANY)
+    part = jax.ShapeDtypeStruct((groups, piece_rows, width), jnp.bfloat16)
+    pieces = (groups, piece_rows, model_width)
+    return pl.pallas_call(
+        arrive_kernel,
+        out_shape=(part, part, part, jax.ShapeDtypeStruct((groups, piece_rows, heads), jnp.float32)),
+        in_specs=[smem, hbm, vmem, hbm, vmem, vmem],
+        out_specs=[vmem] * 4,
+        scratch_shapes=[
+            pltpu.VMEM(pieces, jnp.bfloat16),
+            pltpu.VMEM(pieces, jnp.bfloat16),
+            pltpu.VMEM(pieces, jnp.bfloat16),
+            pltpu.VMEM(weight.shape, jnp.bfloat16),
+            pltpu.VMEM((4 * piece_rows, model_width), jnp.bfloat16),
+            pltpu.SemaphoreType.DMA,
+            pltpu.SemaphoreType.DMA,
+            pltpu.SemaphoreType.DMA((groups,)),
+            pltpu.SemaphoreType.DMA((groups,)),
+        ],
+        compiler_params=pltpu.CompilerParams(
+            collective_id=0, has_side_effects=True, vmem_limit_bytes=50 << 20
+        ),
+    )(sent, tokens.reshape(pieces), gain.reshape(1, -1), weight, beta, bias.reshape(1, -1))
+
 
 PIECE = 48
 SUB = 12
@@ -157,7 +274,161 @@
     )(slot_source, starts, place, q, k, v, logits, sums)
 
 
-rms_epsilon = 1e-06
+def return_kernel(
+    slot_for, out_ref, carry_ref, state_ref, decay_ref, weight, result,
+    chain_send, chain_recv, send, recv, weight_held, gathered, projected,
+    weight_sem, chain_send_sem, chain_recv_sem, send_sem, recv_sem, result_sem,
+):
+    groups, piece_rows, width = send.shape
+    heads, size, _ = state_ref.shape
+    me, seq = lax.axis_index("dp"), lax.axis_index("seq")
+    peers = lax.axis_size("seq")
+    following, previous = lax.rem(seq + 1, peers), lax.rem(seq + peers - 1, peers)
+    weight_copy = pltpu.make_async_copy(weight, weight_held, weight_sem)
+    weight_copy.start()
+    barrier = pltpu.get_barrier_semaphore()
+    greet_group(barrier, groups)
+    pl.semaphore_signal(barrier, inc=1, device_id=(me, following), device_id_type=MESH)
+    pl.semaphore_signal(barrier, inc=1, device_id=(me, previous), device_id_type=MESH)
+
+    @pl.when(seq == 0)
+    def _():
+        chain_recv[...] = jnp.zeros_like(chain_recv)
+
+    pl.semaphore_wait(barrier, groups + 1)
+    links = [
+        pltpu.make_async_remote_copy(
+            src_ref=chain_send.at[h], dst_ref=chain_recv.at[h], send_sem=chain_send_sem.at[h],
+            recv_sem=chain_recv_sem.at[h], device_id=(me, following), device_id_type=MESH,
+        )
+        for h in range(heads)
+    ]
+    for h in range(heads):
+        @pl.when(seq > 0)
+        def _():
+            links[h].wait_recv()
+
+        @pl.when(seq < peers - 1)
+        def _():
+            before = chain_recv[h].astype(jnp.float32)
+            chain_send[h] = (before * decay_ref[h : h + 1, :] + state_ref[h]).astype(jnp.bfloat16)
+            links[h].start()
+
+    def finished(target):
+        slot = slot_for[target]
+        for h in range(heads):
+            cols = slice(h * size, (h + 1) * size)
+            yield cols, (
+                out_ref[slot, :, cols] + dot_nt(carry_ref[slot, :, cols], chain_recv[h])
+            ).astype(jnp.bfloat16)
+
+    copies = []
+    for offset in ORDER:
+        target = peer_along(offset, 1)
+        for cols, part in finished(target):
+            send[target, :, cols] = part
+        copy = pltpu.make_async_remote_copy(
+            src_ref=send.at[target], dst_ref=recv.at[me], send_sem=send_sem.at[target],
+            recv_sem=recv_sem.at[me], device_id=(target, seq), device_id_type=MESH,
+        )
+        copy.start()
+        copies.append(copy)
+    for cols, part in finished(me):
+        recv[me, :, cols] = part
+    weight_copy.wait()
+    sources = [me] + [peer_along(offset, -1) for offset in ORDER]
+    together = gathered.shape[0] // piece_rows
+    model_width = weight_held.shape[1]
+    results = []
+    for first in range(0, groups, together):
+        for n in range(together):
+            source = sources[first + n]
+            if first + n > 0:
+                pltpu.make_async_remote_copy(
+                    src_ref=send.at[source], dst_ref=recv.at[source], send_sem=send_sem.at[source],
+                    recv_sem=recv_sem.at[source], device_id=(source, seq), device_id_type=MESH,
+                ).wait_recv()
+            gathered[n * piece_rows : (n + 1) * piece_rows, :] = recv[source]
+        tile = 512
+        for start in range(0, model_width, tile):
+            cols = slice(start, start + tile)
+            product = jnp.dot(
+                gathered[...], weight_held[:, cols], preferred_element_type=jnp.float32
+            ).astype(jnp.bfloat16)
+            for n in range(together):
+                projected[sources[first + n], :, cols] = product[
+                    n * piece_rows : (n + 1) * piece_rows
+                ]
+        for n in range(together):
+            source = sources[first + n]
+            copy = pltpu.make_async_copy(
+                projected.at[source], result.at[source], result_sem.at[source]
+            )
+            copy.start()
+            results.append(copy)
+    for copy in results:
+        copy.wait()
+    for copy in copies:
+        copy.wait_send()
+    for h in range(heads):
+        @pl.when(seq < peers - 1)
+        def _():
+            links[h].wait_send()
+
+
+def give_back(slot_for, out, carry, state, decay, weight):
+    groups = slot_for.shape[0]
+    rows, width = out.shape
+    piece_rows = rows // groups
+    heads, size, _ = state.shape
+    model_width = weight.shape[1]
+    smem = pl.BlockSpec(memory_space=pltpu.SMEM)
+    vmem = pl.BlockSpec(memory_space=pltpu.VMEM)
+    hbm = pl.BlockSpec(memory_space=pl.ANY)
+    pieces = (groups, piece_rows, width)
+    return pl.pallas_call(
+        return_kernel,
+        out_shape=jax.ShapeDtypeStruct((groups, piece_rows, model_width), jnp.bfloat16),
+        in_specs=[smem, vmem, vmem, vmem, vmem, hbm],
+        out_specs=hbm,
+        scratch_shapes=[
+            pltpu.VMEM((heads, size, size), jnp.bfloat16),
+            pltpu.VMEM((heads, size, size), jnp.bfloat16),
+            pltpu.VMEM(pieces, jnp.bfloat16),
+            pltpu.VMEM(pieces, jnp.bfloat16),
+            pltpu.VMEM(weight.shape, jnp.bfloat16),
+            pltpu.VMEM((4 * piece_rows, width), jnp.bfloat16),
+            pltpu.VMEM((groups, piece_rows, model_width), jnp.bfloat16),
+            pltpu.SemaphoreType.DMA,
+            pltpu.SemaphoreType.DMA((heads,)),
+            pltpu.SemaphoreType.DMA((heads,)),
+            pltpu.SemaphoreType.DMA((groups,)),
+            pltpu.SemaphoreType.DMA((groups,)),
+            pltpu.SemaphoreType.DMA((groups,)),
+        ],
+        compiler_params=pltpu.CompilerParams(
+            collective_id=1, has_side_effects=True, vmem_limit_bytes=50 << 20
+        ),
+    )(slot_for, out.reshape(pieces), carry.reshape(pieces), state, decay, weight)
+
+
+def place_kernel(target_for, projected, result):
+    result[...] = projected[...]
+
+
+def place_pieces(target_for, projected):
+    groups, piece_rows, model_width = projected.shape
+    block = (1, piece_rows, model_width)
+    return pl.pallas_call(
+        place_kernel,
+        out_shape=jax.ShapeDtypeStruct(projected.shape, projected.dtype),
+        grid_spec=pltpu.PrefetchScalarGridSpec(
+            num_scalar_prefetch=1,
+            grid=(groups,),
+            in_specs=[pl.BlockSpec(block, lambda n, target_for: (target_for[n], 0, 0))],
+            out_specs=pl.BlockSpec(block, lambda n, target_for: (n, 0, 0)),
+        ),
+    )(target_for, projected)
 
 
 def shards(
@@ -176,48 +447,20 @@
     seq_index = lax.axis_index("seq")
     tok_dev, model_width = tokens.shape
     piece_rows = tok_dev // groups
-    head_count = beta_weight.shape[1]
-    head_size = qkv_weight.shape[2] // head_count
     plan_source = lax.dynamic_index_in_dim(source_dp, seq_index, 1, keepdims=False)
     plan_offset = lax.dynamic_index_in_dim(source_offset, seq_index, 1, keepdims=False)
     from_here = plan_source == dp_index
     sent_piece = jnp.sum(jnp.where(from_here, plan_offset, 0), axis=1) // piece_rows
-    outgoing = tokens.reshape(groups, piece_rows, model_width)[sent_piece]
-    incoming = lax.all_to_all(outgoing, "dp", split_axis=0, concat_axis=0, tiled=True)
     slot_source = lax.dynamic_index_in_dim(plan_source, dp_index, 0, keepdims=False)
-    owned = incoming.reshape(tok_dev, model_width)
-    rows_float = owned.astype(jnp.float32)
-    normed = (
-        rows_float
-        * lax.rsqrt(jnp.mean(rows_float * rows_float, axis=1, keepdims=True) + rms_epsilon)
-        * norm_gain
-    ).astype(jnp.bfloat16)
-    query_rows, key_rows, value_rows = (
-        jnp.dot(normed, qkv_weight[n], preferred_element_type=jnp.float32)
-        .astype(jnp.bfloat16)
-        .reshape(groups, piece_rows, -1)
-        for n in range(3)
+    query_rows, key_rows, value_rows, logits = arrive(
+        sent_piece, tokens, norm_gain, qkv_weight, beta_weight, beta_bias
     )
-    logits = jnp.dot(normed, beta_weight, preferred_element_type=jnp.float32) + beta_bias
-    logits = logits.reshape(groups, piece_rows, head_count)
     lengths = lax.dynamic_index_in_dim(doc_lengths, dp_index, 0, keepdims=False)
     starts = jnp.cumsum(lengths) - lengths
     place = (seq_index * tok_dev).astype(jnp.int32).reshape(1)
     heads_out, carried, local_state, decay_all = recurrence(
         slot_source, starts, place, query_rows, key_rows, value_rows, logits
     )
-    all_decay = lax.all_gather(decay_all, "seq")
-    all_state = lax.all_gather(local_state, "seq")
-    before = jnp.zeros_like(local_state)
-    for k in range(lax.axis_size("seq") - 1):
-        before = jnp.where(k < seq_index, before * all_decay[k][:, None, :] + all_state[k], before)
-    heads_out = heads_out.reshape(tok_dev, head_count, head_size) + jnp.einsum(
-        "thj,hij->thi",
-        carried.reshape(tok_dev, head_count, head_size),
-        before.astype(jnp.bfloat16),
-        preferred_element_type=jnp.float32,
-    )
-    attended = heads_out.reshape(tok_dev, head_count * head_size).astype(jnp.bfloat16)
     numbers = jnp.arange(groups, dtype=jnp.int32)
     slot_for = jnp.sum(
         jnp.where(slot_source[None, :] == numbers[:, None], numbers[None, :], 0), axis=1
@@ -225,15 +468,8 @@
     target_for = jnp.sum(
         jnp.where(sent_piece[None, :] == numbers[:, None], numbers[None, :], 0), axis=1
     )
-    returned = lax.all_to_all(
-        attended.reshape(groups, piece_rows, -1)[slot_for],
-        "dp",
-        split_axis=0,
-        concat_axis=0,
-        tiled=True,
-    )
-    returned = returned[target_for].reshape(tok_dev, -1)
-    return jnp.dot(returned, out_weight, preferred_element_type=jnp.float32).astype(jnp.bfloat16)
+    projected = give_back(slot_for, heads_out, carried, local_state, decay_all, out_weight)
+    return place_pieces(target_for, projected).reshape(tok_dev, model_width)
 
 
 def solution(mesh):

time: 233 us -> 149 us (0.64)
  Pallas kernels: 33.5 us -> 137 us
  waiting for transfers between devices: 84.1 us -> 0 us
  matrix products: 30.8 us -> 0 us
  local copies, waits for them, and re-layouts: 30.2 us -> 9.57 us
  starting transfers between devices: 15 us -> 0 us
  between operations: 13.6 us -> 0.07 us
  blocking collectives: 13 us -> 0 us
  other arithmetic: 9.97 us -> 2.16 us
    pallas_call x0 -> x3, Pallas kernels: none -> 103 us  [the longest x1 48.7 us: arrive(): pl.pallas_call(arrive_kernel, out_shape=(part, part, part, jax.ShapeDtype...]
    all_to_all x2 -> x0, waiting for transfers between devices: 71.7 us -> none  [the longest x1 46.4 us: shards(): lax.all_to_all(outgoing, 'dp', split_axis=0, concat_axis=0, tiled=True)]
    dot_general x6 -> x0, matrix products: 30.8 us -> none  [the longest x3 16 us: shards(): jnp.dot(normed, qkv_weight[n], preferred_element_type=jnp.float32)]
    all_to_all x2 -> x0, starting transfers between devices: 15 us -> none  [the longest x1 8.05 us: shards(): lax.all_to_all(outgoing, 'dp', split_axis=0, concat_axis=0, tiled=True)]
    all_gather x1 -> x0, blocking collectives: 13 us -> none  [shards(): all_decay = lax.all_gather(decay_all, 'seq')]
    all_gather x1 -> x0, waiting for transfers between devices: 12.4 us -> none  [shards(): all_state = lax.all_gather(local_state, 'seq')]
    gather x3 -> x0, local copies, waits for them, and re-layouts: 8.83 us -> none  [the longest x1 3.21 us: shards(): returned = returned[target_for].reshape(tok_dev, -1)]
    convert_element_type x2 -> x0, local copies, waits for them, and re-layouts: 6.63 us -> none  [shards(): heads_out.reshape(tok_dev, head_count * head_size).astype(jnp.bfloat16)]
  transfers between devices with their start and end apart: 3 -> 0, of which waited for: 3 -> 0; matrix products, arithmetic and copies ran while one was open for 2% -> 0% of each run, Pallas kernels for 0% -> 0%
where the time goes in v2:
time: 149 us; the launch traced here: 148 us
  Pallas kernels  137 us (92%)
  local copies, waits for them, and re-layouts  9.57 us (6%)
  other arithmetic  2.16 us (1%)
    pallas_call x1, Pallas kernels, arrive(): pl.pallas_call(arrive_kernel, out_shape=(part, part, part, jax.ShapeDtype...  48.7 us
    pallas_call x1, Pallas kernels, give_back(): pl.pallas_call(return_kernel, out_shape=jax.ShapeDtypeStruct((groups, pie...  43.6 us
    pallas_call x1, Pallas kernels, recurrence(): pl.pallas_call(recurrence_kernel, out_shape=(jax.ShapeDtypeStruct((pieces...  33.7 us
    pallas_call x1, Pallas kernels, place_pieces(): pl.pallas_call(place_kernel, out_shape=jax.ShapeDtypeStruct(projected.sha...  10.5 us
    unnamed x17, local copies, waits for them, and re-layouts  8.7 us

profile of v2, /device:TPU:24, one launch (start us, length us, event | category | flops | bytes accessed | tf_op | source)
XLA Modules:
  0.0 148.3 jit_solution(13645845467460784891)
XLA Ops:
  0.0 0.0 copy-start
  0.0 0.7 copy-done
  0.7 0.2 dynamic-slice_reduce_fusion
  0.9 0.2 reduce-window.9
  1.1 0.7 fusion.1.slot_source
  1.8 1.2 fusion
  3.0 1.0 copy.12.beta_ref
  4.1 0.0 copy-start.6
  4.1 0.7 copy-done.6
  4.8 0.0 copy-start.7
  4.8 0.7 copy-done.7
  5.4 0.0 copy-start.5
  5.4 48.7 %shard_map.100 = (bf16[16,48,1024]{2,1,0:T(8,128)(2,1)S(1)}, bf16[16,48,1024]{2,1,0:T(8,128)(2,1)S(1)}, bf16[16,48,1024]{2,1,0:T(8,128)(2,1)}, f32[16,48,8]{2,1,0:T(8,128)S(1)}) custom-call(s32[16]{0:T(128)S(1)} %and_select_fusion.sent, bf16[16,48,2048]{2,1,0:T(8,128)(2,1)} %bitcast.16, f32[1,2048]{1,0:T(1,128)S(1)} %bitcast.14, ...), custom_call_target="tpu_custom_call" | custom-call | tf_op jit(solution)/shard_map/pallas_call | solution.py:104
  54.2 0.0 copy-start.2
  54.2 1.1 copy-done.2
  55.3 0.0 copy-done.5
  55.3 0.0 copy-start.3
  55.3 1.4 copy-done.3
  56.7 0.0 copy-start.4
  56.7 1.4 copy-done.4
  58.1 33.7 %shard_map.101 = (f32[768,1024]{1,0:T(8,128)S(1)}, bf16[768,1024]{1,0:T(8,128)(2,1)S(1)}, f32[8,128,128]{2,1,0:T(8,128)S(1)}, f32[8,128]{1,0:T(8,128)S(1)}) custom-call(s32[16]{0:T(128)S(1)} %fusion.1.slot_source, s32[8]{0:T(128)S(1)} %bitcast_subtract_fusion.starts, s32[1]{0:T(128)} %bitcast.2.place, bf16[16,48,1024]{2,1,0:T(8,128)(2,1)S(1)} %get-tuple-element.13.q_ref, ...), custom_call_target="tpu_custom_call" | custom-call | tf_op jit(solution)/shard_map/pallas_call | solution.py:259
  91.9 0.0 copy-start.1
  91.9 1.7 %copy-done.1 = f32[768,1024]{1,0:T(8,128)} copy-done((f32[768,1024]{1,0:T(8,128)}, f32[768,1024]{1,0:T(8,128)S(1)}, u32[]{:S(2)}) %copy-start.1) | copy-done | bytes 3145752
  93.6 0.1 select_reduce_fusion.slot_for
  93.7 43.6 %shard_map.102.projected = bf16[16,48,2048]{2,1,0:T(8,128)(2,1)} custom-call(s32[16]{0:T(128)S(1)} %select_reduce_fusion.slot_for, f32[16,48,1024]{2,1,0:T(8,128)} %bitcast.12, bf16[16,48,1024]{2,1,0:T(8,128)(2,1)S(1)} %bitcast.13, f32[8,128,128]{2,1,0:T(8,128)S(1)} %get-tuple-element.19.state_ref, f32[8,128]{1,0:T(8,128)S(1)} %get-tuple-element.20.decay_ref, ...), custom_call_target="tpu_custom_call" | custom-call | tf_op jit(solution)/shard_map/pallas_call | solution.py:389
  137.2 0.6 select_reduce_fusion.1.target_for
  137.8 10.5 %shard_map.103 = bf16[16,48,2048]{2,1,0:T(8,128)(2,1)} custom-call(s32[16]{0:T(128)} %select_reduce_fusion.1.target_for, bf16[16,48,2048]{2,1,0:T(8,128)(2,1)} %shard_map.102.projected), custom_call_target="tpu_custom_call" | custom-call | tf_op jit(solution)/shard_map/pallas_call | solution.py:422
  (2 shorter events, 0.0 us)
Async XLA Ops:
  0.0 0.7 copy-start
  4.1 0.7 copy-start.6
  4.8 0.7 copy-start.7
  5.4 49.9 %copy-start.5 = (bf16[240,96]{1,0:T(8,128)(2,1)S(1)}, bf16[240,96]{1,0:T(8,128)(2,1)}, u32[]{:S(2)}) copy-start(bf16[240,96]{1,0:T(8,128)(2,1)} %constant.62.clone.sums_ref) | copy-start | bytes 138244
  54.2 1.1 copy-start.2
  55.3 1.4 copy-start.3
  56.7 1.4 copy-start.4
  91.9 1.7 %copy-start.1 = (f32[768,1024]{1,0:T(8,128)}, f32[768,1024]{1,0:T(8,128)S(1)}, u32[]{:S(2)}) copy-start(f32[768,1024]{1,0:T(8,128)S(1)} %get-tuple-element.17) | copy-start | bytes 9437188

commit v3 on v1

v3 whole, which is shorter than its diff:
```python
import jax
import jax.numpy as jnp
import numpy as np
from jax import lax
from jax.experimental import pallas as pl
from jax.experimental.pallas import tpu as pltpu
from jax.sharding import PartitionSpec as P

PIECE = 48
SUB = 12
TOGETHER = 4
MESH = pl.DeviceIdType.MESH
rms_epsilon = 1e-06
ORDER = [(1, 0), (3, 3), (2, 3), (1, 3), (1, 2), (0, 1), (2, 0), (3, 0), (3, 1), (2, 2), (0, 2), (3, 2), (1, 1), (0, 3), (2, 1)]


def decay_sums():
    row = np.arange(PIECE)[:, None]
    col = np.arange(PIECE)[None, :]

    def between(low, high):
        return ((col > low) & (col <= high)).astype(np.float32)

    mid = (row // SUB) * SUB + SUB // 2 - 1
    near = between(mid, row) - between(row, mid)
    half = (row // (2 * SUB)) * (2 * SUB) + SUB - 1
    pair = between(half, row) + between(row, half)
    middle = np.full_like(row, 2 * SUB - 1)
    whole = between(middle, row) + between(row, middle)
    before = between(np.full_like(row, -1), row)
    after = between(row, np.full_like(row, PIECE - 1))
    sums = np.concatenate([near, pair, whole, before, after], axis=0)
    return np.concatenate([sums, sums], axis=1)


def dot_nt(a, b):
    return lax.dot_general(a, b, (((1,), (1,)), ((), ())), preferred_element_type=jnp.float32)


def dot_tn(a, b):
    return lax.dot_general(a, b, (((0,), (0,)), ((), ())), preferred_element_type=jnp.float32)


def peer_along(offset, sign):
    me = lax.axis_index("dp")
    down, right = offset
    row = lax.rem(me // 4 + (down if sign > 0 else 4 - down), 4)
    column = lax.rem(lax.rem(me, 4) + (right if sign > 0 else 4 - right), 4)
    return row * 4 + column


def layer_kernel(
    sent, slot_of, rank_of, starts, tokens, gain_ref, weight, beta_ref, bias_ref, sums_ref,
    out_weight, result,
    held, send, recv, weight_held, out_weight_held, normed, qkv, strength_ref,
    out_ref, carry_ref, change_ref, decay_ref, state, total, prefix_ref, totals_ref,
    chain_send, chain_recv, back_send, back_recv, gathered,
    token_sem, weight_sem, out_weight_sem, send_sem, recv_sem,
    chain_send_sem, chain_recv_sem, back_send_sem, back_recv_sem, result_sem,
):
    groups, piece_rows, model_width = held.shape
    heads, size, _ = state.shape
    width = heads * size
    me, seq = lax.axis_index("dp"), lax.axis_index("seq")
    peers = lax.axis_size("seq")
    following, previous = lax.rem(seq + 1, peers), lax.rem(seq + peers - 1, peers)
    token_copy = pltpu.make_async_copy(tokens, held, token_sem)
    token_copy.start()
    weight_copy = pltpu.make_async_copy(weight, weight_held, weight_sem)
    out_weight_copy = pltpu.make_async_copy(out_weight, out_weight_held, out_weight_sem)
    barrier = pltpu.get_barrier_semaphore()
    for distance in range(1, groups):
        pl.semaphore_signal(
            barrier, inc=1, device_id=(lax.rem(me + distance, groups), seq), device_id_type=MESH
        )
    pl.semaphore_signal(barrier, inc=1, device_id=(me, following), device_id_type=MESH)
    pl.semaphore_signal(barrier, inc=1, device_id=(me, previous), device_id_type=MESH)
    token_copy.wait()
    weight_copy.start()
    out_weight_copy.start()
    send[0] = held[sent[me]]
    own_copy = pltpu.make_async_copy(send.at[0], recv.at[0], recv_sem.at[0])
    own_copy.start()

    @pl.when(seq == 0)
    def _():
        chain_recv[...] = jnp.zeros_like(chain_recv)

    pl.semaphore_wait(barrier, groups + 1)
    copies = []
    for n, offset in enumerate(ORDER):
        target = peer_along(offset, 1)
        send[n + 1] = held[sent[target]]
        copy = pltpu.make_async_remote_copy(
            src_ref=send.at[n + 1], dst_ref=recv.at[n + 1], send_sem=send_sem.at[n + 1],
            recv_sem=recv_sem.at[n + 1], device_id=(target, seq), device_id_type=MESH,
        )
        copy.start()
        copies.append(copy)
    weight_copy.wait()

    down = lax.broadcasted_iota(jnp.int32, (PIECE, PIECE), 0)
    across = lax.broadcasted_iota(jnp.int32, (PIECE, PIECE), 1)
    wide = lax.broadcasted_iota(jnp.int32, (PIECE, size), 0)
    causal = down >= across
    in_sub = causal & (down // SUB == across // SUB)
    in_pair = causal & (down // (2 * SUB) == across // (2 * SUB)) & (down // SUB != across // SUB)
    in_whole = causal & (down // (2 * SUB) != across // (2 * SUB))
    right_pair = (wide // SUB) % 2 == 1
    right_whole = wide >= 2 * SUB

    def document_of(position):
        count = jnp.zeros_like(position)
        for n in range(starts.shape[0]):
            count = count + (starts[n] <= position).astype(jnp.int32)
        return count

    def local_part(inside, rank):
        first = (seq * groups + slot_of[rank]) * PIECE
        doc_down = document_of(first + down)
        doc_across = document_of(first + across)
        doc_wide = document_of(first + wide)
        doc_before = document_of(first - 1)
        doc_last = document_of(first + PIECE - 1)
        same = doc_down == doc_across
        near_mask, pair_mask, whole_mask = in_sub & same, in_pair & same, in_whole & same
        reaches = (doc_wide == doc_before).astype(jnp.float32)
        stays = (doc_wide == doc_last).astype(jnp.float32)
        kept = (doc_last == doc_before).astype(jnp.float32)
        strength = strength_ref[inside]
        for h in range(heads):
            cols = slice(h * size, (h + 1) * size)
            query = qkv[0, inside, :, cols].astype(jnp.float32)
            key = qkv[1, inside, :, cols].astype(jnp.float32)
            value = qkv[2, inside, :, cols].astype(jnp.float32)
            squares = key * key
            now = strength[:, h : h + 1]
            step = now / (1.0 + now * jnp.sum(squares, axis=1, keepdims=True))
            log_decay = jnp.log(1.0 - step * squares)
            high = log_decay.astype(jnp.bfloat16)
            low = (log_decay - high.astype(jnp.float32)).astype(jnp.bfloat16)
            gaps = jnp.dot(
                sums_ref[...], jnp.concatenate([high, low], axis=0),
                preferred_element_type=jnp.float32,
            )
            near = gaps[:PIECE]
            pair = gaps[PIECE : 2 * PIECE]
            whole = gaps[2 * PIECE : 3 * PIECE]
            before = gaps[3 * PIECE : 4 * PIECE]
            after = gaps[4 * PIECE :]
            near_query = (query * jnp.exp(near)).astype(jnp.bfloat16)
            near_key = (key * jnp.exp(-near)).astype(jnp.bfloat16)
            pair_both = (jnp.where(right_pair, query, key) * jnp.exp(pair)).astype(jnp.bfloat16)
            whole_both = (jnp.where(right_whole, query, key) * jnp.exp(whole)).astype(jnp.bfloat16)
            scores = jnp.where(
                near_mask,
                dot_nt(near_query, near_key),
                jnp.where(
                    pair_mask,
                    dot_nt(pair_both, pair_both),
                    jnp.where(whole_mask, dot_nt(whole_both, whole_both), 0.0),
                ),
            )
            stepped = (value * step).astype(jnp.bfloat16)
            decayed = jnp.exp(before)
            out_ref[rank, :, cols] = jnp.dot(
                scores.astype(jnp.bfloat16), stepped, preferred_element_type=jnp.float32
            )
            carry_ref[rank, :, cols] = (query * (decayed * reaches)).astype(jnp.bfloat16)
            decay_ref[rank, h : h + 1, :] = decayed[PIECE - 1 :, :] * kept
            change_ref[rank, h] = dot_tn(
                stepped, (key * (jnp.exp(after) * stays)).astype(jnp.bfloat16)
            )

    @pl.loop(0, groups // TOGETHER)
    def _(group):
        for n in range(TOGETHER):
            rank = group * TOGETHER + n
            pltpu.make_async_copy(send.at[rank], recv.at[rank], recv_sem.at[rank]).wait()
            rows = recv[rank].astype(jnp.float32)
            normed[n * PIECE : (n + 1) * PIECE, :] = (
                rows
                * lax.rsqrt(jnp.mean(rows * rows, axis=1, keepdims=True) + rms_epsilon)
                * gain_ref[...]
            ).astype(jnp.bfloat16)
        logits = (
            jnp.dot(normed[...], beta_ref[...], preferred_element_type=jnp.float32) + bias_ref[...]
        )
        strength = 1.0 / (1.0 + jnp.exp(-logits))
        for n in range(TOGETHER):
            strength_ref[n] = strength[n * PIECE : (n + 1) * PIECE]
        tile = 512
        for part in range(3):
            for start in range(0, width, tile):
                cols = slice(start, start + tile)
                product = jnp.dot(
                    normed[...], weight_held[part, :, cols], preferred_element_type=jnp.float32
                ).astype(jnp.bfloat16)
                for n in range(TOGETHER):
                    qkv[part, n, :, cols] = product[n * PIECE : (n + 1) * PIECE]

        @pl.loop(0, TOGETHER)
        def _(inside):
            local_part(inside, group * TOGETHER + inside)

    state[...] = jnp.zeros_like(state)
    total[...] = jnp.ones_like(total)

    @pl.loop(0, groups)
    def _(slot):
        rank = rank_of[slot]
        for h in range(heads):
            prefix_ref[slot, h] = state[h].astype(jnp.bfloat16)
            state[h] = state[h] * decay_ref[rank, h : h + 1, :] + change_ref[rank, h]
        totals_ref[slot] = total[...]
        total[...] = total[...] * decay_ref[rank]

    def add_earlier(rank):
        slot = slot_of[rank]
        for h in range(heads):
            cols = slice(h * size, (h + 1) * size)
            carried = carry_ref[rank, :, cols]
            out_ref[rank, :, cols] += dot_nt(carried, prefix_ref[slot, h])
            carry_ref[rank, :, cols] = (
                carried.astype(jnp.float32) * totals_ref[slot, h : h + 1, :]
            ).astype(jnp.bfloat16)

    ahead = 2 * (seq + 1)
    pl.loop(0, ahead)(add_earlier)
    links = [
        pltpu.make_async_remote_copy(
            src_ref=chain_send.at[h], dst_ref=chain_recv.at[h], send_sem=chain_send_sem.at[h],
            recv_sem=chain_recv_sem.at[h], device_id=(me, following), device_id_type=MESH,
        )
        for h in range(heads)
    ]
    for h in range(heads):
        @pl.when(seq > 0)
        def _():
            links[h].wait_recv()

        @pl.when(seq < peers - 1)
        def _():
            before = chain_recv[h].astype(jnp.float32)
            chain_send[h] = (before * total[h : h + 1, :] + state[h]).astype(jnp.bfloat16)
            links[h].start()

    pl.loop(ahead, groups)(add_earlier)

    def finished(rank):
        for h in range(heads):
            cols = slice(h * size, (h + 1) * size)
            yield cols, (
                out_ref[rank, :, cols] + dot_nt(carry_ref[rank, :, cols], chain_recv[h])
            ).astype(jnp.bfloat16)

    for n, offset in enumerate(ORDER):
        for cols, part in finished(n + 1):
            back_send[n + 1, :, cols] = part
        copy = pltpu.make_async_remote_copy(
            src_ref=back_send.at[n + 1], dst_ref=back_recv.at[n + 1],
            send_sem=back_send_sem.at[n + 1], recv_sem=back_recv_sem.at[n + 1],
            device_id=(peer_along(offset, -1), seq), device_id_type=MESH,
        )
        copy.start()
        copies.append(copy)
    for cols, part in finished(0):
        back_send[0, :, cols] = part
    own_back = pltpu.make_async_copy(back_send.at[0], back_recv.at[0], back_recv_sem.at[0])
    own_back.start()
    out_weight_copy.wait()

    @pl.loop(0, groups // TOGETHER)
    def _(group):
        for n in range(TOGETHER):
            rank = group * TOGETHER + n
            pltpu.make_async_copy(
                back_send.at[rank], back_recv.at[rank], back_recv_sem.at[rank]
            ).wait()
            gathered[n * PIECE : (n + 1) * PIECE, :] = back_recv[rank]
        tile = 512
        for start in range(0, model_width, tile):
            cols = slice(start, start + tile)
            product = jnp.dot(
                gathered[...], out_weight_held[:, cols], preferred_element_type=jnp.float32
            ).astype(jnp.bfloat16)
            for n in range(TOGETHER):
                held[group * TOGETHER + n, :, cols] = product[n * PIECE : (n + 1) * PIECE]
        for n in range(TOGETHER):
            rank = group * TOGETHER + n
            pltpu.make_async_copy(held.at[rank], result.at[rank], result_sem.at[rank]).start()

    for rank in range(groups):
        pltpu.make_async_copy(held.at[rank], result.at[rank], result_sem.at[rank]).wait()
    for copy in copies:
        copy.wait_send()

    @pl.when(seq < peers - 1)
    def _():
        for link in links:
            link.wait_send()


def layer(sent, slot_of, rank_of, starts, tokens, gain, weight, beta, bias, out_weight):
    groups = sent.shape[0]
    rows, model_width = tokens.shape
    width = weight.shape[2]
    heads = beta.shape[1]
    size = width // heads
    smem = pl.BlockSpec(memory_space=pltpu.SMEM)
    vmem = pl.BlockSpec(memory_space=pltpu.VMEM)
    hbm = pl.BlockSpec(memory_space=pl.ANY)
    pieces = (groups, PIECE, model_width)
    narrow = (groups, PIECE, width)
    states = (heads, size, size)
    bfloat16, float32 = jnp.bfloat16, jnp.float32
    sems = pltpu.SemaphoreType.DMA((groups,))
    head_sems = pltpu.SemaphoreType.DMA((heads,))
    sums = jnp.asarray(decay_sums(), bfloat16)
    return pl.pallas_call(
        layer_kernel,
        out_shape=jax.ShapeDtypeStruct(pieces, bfloat16),
        in_specs=[smem] * 4 + [hbm, vmem, hbm, vmem, vmem, vmem, hbm],
        out_specs=hbm,
        scratch_shapes=[
            pltpu.VMEM(pieces, bfloat16),
            pltpu.VMEM(pieces, bfloat16),
            pltpu.VMEM(pieces, bfloat16),
            pltpu.VMEM(weight.shape, bfloat16),
            pltpu.VMEM(out_weight.shape, bfloat16),
            pltpu.VMEM((TOGETHER * PIECE, model_width), bfloat16),
            pltpu.VMEM((3, TOGETHER, PIECE, width), bfloat16),
            pltpu.VMEM((TOGETHER, PIECE, heads), float32),
            pltpu.VMEM(narrow, float32),
            pltpu.VMEM(narrow, bfloat16),
            pltpu.VMEM((groups,) + states, float32),
            pltpu.VMEM((groups, heads, size), float32),
            pltpu.VMEM(states, float32),
            pltpu.VMEM((heads, size), float32),
            pltpu.VMEM((groups,) + states, bfloat16),
            pltpu.VMEM((groups, heads, size), float32),
            pltpu.VMEM(states, bfloat16),
            pltpu.VMEM(states, bfloat16),
            pltpu.VMEM(narrow, bfloat16),
            pltpu.VMEM(narrow, bfloat16),
            pltpu.VMEM((TOGETHER * PIECE, width), bfloat16),
            pltpu.SemaphoreType.DMA,
            pltpu.SemaphoreType.DMA,
            pltpu.SemaphoreType.DMA,
            sems,
            sems,
            head_sems,
            head_sems,
            sems,
            sems,
            sems,
        ],
        compiler_params=pltpu.CompilerParams(
            collective_id=0, has_side_effects=True, vmem_limit_bytes=60 << 20
        ),
    )(
        sent, slot_of, rank_of, starts, tokens.reshape(pieces), gain.reshape(1, -1), weight, beta,
        bias.reshape(1, -1), sums, out_weight,
    )


def place_kernel(rank_for, projected, result, held, in_sems, out_sems):
    pieces = projected.shape[0]
    arrive = [
        pltpu.make_async_copy(projected.at[rank_for[n]], held.at[n], in_sems.at[n])
        for n in range(pieces)
    ]
    leave = [
        pltpu.make_async_copy(held.at[n], result.at[n], out_sems.at[n]) for n in range(pieces)
    ]
    for copy in arrive:
        copy.start()
    for n in range(pieces):
        arrive[n].wait()
        leave[n].start()
    for copy in leave:
        copy.wait()


def place_pieces(rank_for, projected):
    hbm = pl.BlockSpec(memory_space=pl.ANY)
    sems = pltpu.SemaphoreType.DMA((projected.shape[0],))
    return pl.pallas_call(
        place_kernel,
        out_shape=jax.ShapeDtypeStruct(projected.shape, projected.dtype),
        in_specs=[pl.BlockSpec(memory_space=pltpu.SMEM), hbm],
        out_specs=hbm,
        scratch_shapes=[pltpu.VMEM(projected.shape, projected.dtype), sems, sems],
    )(rank_for, projected)


def shards(
    tokens,
    norm_gain,
    qkv_weight,
    beta_weight,
    beta_bias,
    out_weight,
    doc_lengths,
    source_dp,
    source_offset,
):
    groups = lax.axis_size("dp")
    dp_index = lax.axis_index("dp")
    seq_index = lax.axis_index("seq")
    tok_dev, model_width = tokens.shape
    piece_rows = tok_dev // groups
    plan_source = lax.dynamic_index_in_dim(source_dp, seq_index, 1, keepdims=False)
    plan_offset = lax.dynamic_index_in_dim(source_offset, seq_index, 1, keepdims=False)
    from_here = plan_source == dp_index
    sent = jnp.sum(jnp.where(from_here, plan_offset, 0), axis=1) // piece_rows
    slot_source = lax.dynamic_index_in_dim(plan_source, dp_index, 0, keepdims=False)
    steps = np.asarray([(0, 0)] + ORDER, np.int32)

    def along(sign):
        return (dp_index // 4 + sign * steps[:, 0]) % 4 * 4 + (dp_index + sign * steps[:, 1]) % 4

    numbers = jnp.arange(groups, dtype=jnp.int32)
    from_rank = slot_source[:, None] == along(-1)[None, :]
    slot_of = jnp.sum(jnp.where(from_rank, numbers[:, None], 0), axis=0)
    rank_of = jnp.sum(jnp.where(from_rank, numbers[None, :], 0), axis=1)
    owned_piece = jnp.sum(
        jnp.where(along(1)[:, None] == numbers[None, :], sent[None, :], 0), axis=1
    )
    rank_for = jnp.sum(
        jnp.where(owned_piece[None, :] == numbers[:, None], numbers[None, :], 0), axis=1
    )
    lengths = lax.dynamic_index_in_dim(doc_lengths, dp_index, 0, keepdims=False)
    starts = jnp.cumsum(lengths) - lengths
    projected = layer(
        sent, slot_of, rank_of, starts, tokens, norm_gain, qkv_weight, beta_weight, beta_bias,
        out_weight,
    )
    return place_pieces(rank_for, projected).reshape(tok_dev, model_width)


def solution(mesh):
    return jax.shard_map(
        shards,
        mesh=mesh,
        in_specs=(P(("dp", "seq"), None), P(), P(), P(), P(), P(), P(), P(), P()),
        out_specs=P(("dp", "seq"), None),
        check_vma=False,
    )
```

time: 233 us -> 135 us (0.58)
  Pallas kernels: 33.5 us -> 127 us
  waiting for transfers between devices: 84.1 us -> 0 us
  matrix products: 30.8 us -> 0 us
  local copies, waits for them, and re-layouts: 30.2 us -> 2.66 us
  starting transfers between devices: 15 us -> 0 us
  between operations: 13.6 us -> 0.03 us
  blocking collectives: 13 us -> 0 us
  other arithmetic: 9.97 us -> 4.84 us
    pallas_call x1 -> x2, Pallas kernels: 33.5 us -> 127 us  [the longest x1 123 us: layer(): pl.pallas_call(layer_kernel, out_shape=jax.ShapeDtypeStruct(pieces, bfloa...]
    all_to_all x2 -> x0, waiting for transfers between devices: 71.7 us -> none  [the longest x1 46.4 us: shards(): lax.all_to_all(outgoing, 'dp', split_axis=0, concat_axis=0, tiled=True)]
    dot_general x6 -> x0, matrix products: 30.8 us -> none  [the longest x3 16 us: shards(): jnp.dot(normed, qkv_weight[n], preferred_element_type=jnp.float32)]
    all_to_all x2 -> x0, starting transfers between devices: 15 us -> none  [the longest x1 8.05 us: shards(): lax.all_to_all(outgoing, 'dp', split_axis=0, concat_axis=0, tiled=True)]
    all_gather x1 -> x0, blocking collectives: 13 us -> none  [shards(): all_decay = lax.all_gather(decay_all, 'seq')]
    all_gather x1 -> x0, waiting for transfers between devices: 12.4 us -> none  [shards(): all_state = lax.all_gather(local_state, 'seq')]
    gather x3 -> x0, local copies, waits for them, and re-layouts: 8.83 us -> none  [the longest x1 3.21 us: shards(): returned = returned[target_for].reshape(tok_dev, -1)]
    unnamed x30 -> x5, local copies, waits for them, and re-layouts: 9.34 us -> 1.77 us
  transfers between devices with their start and end apart: 3 -> 0, of which waited for: 3 -> 0; matrix products, arithmetic and copies ran while one was open for 2% -> 0% of each run, Pallas kernels for 0% -> 0%
where the time goes in v3:
time: 135 us; the launch traced here: 134 us
  Pallas kernels  127 us (94%)
  other arithmetic  4.84 us (4%)
  local copies, waits for them, and re-layouts  2.66 us (2%)
    pallas_call x1, Pallas kernels, layer(): pl.pallas_call(layer_kernel, out_shape=jax.ShapeDtypeStruct(pieces, bfloa...  123 us
    pallas_call x1, Pallas kernels, place_pieces(): pl.pallas_call(place_kernel, out_shape=jax.ShapeDtypeStruct(projected.sha...  3.84 us

profile of v3, /device:TPU:24, one launch (start us, length us, event | category | flops | bytes accessed | tf_op | source)
XLA Modules:
  0.0 134.2 jit_solution(887691197731905062)
XLA Ops:
  0.0 0.0 copy-start
  0.0 0.7 fusion.11
  0.7 1.2 fusion.2
  2.0 0.0 copy-done
  2.0 0.2 dynamic-slice_reduce_fusion
  2.2 0.7 fusion.4
  2.8 0.7 and_select_fusion.2
  3.5 0.0 copy-start.1
  3.5 0.2 select_reduce_fusion.1
  3.7 0.6 select_reduce_fusion.rank_for
  4.3 0.8 fusion.1
  5.1 0.2 reduce-window.9
  5.3 0.5 bitcast_subtract_fusion.starts
  5.8 1.8 %copy.16.beta_ref = bf16[2048,8]{1,0:T(8,128)(2,1)} copy(bf16[2048,8]{0,1:T(8,128)(2,1)} %param.17) | data formatting | bytes 65536 | tf_op args[3]
  7.5 0.0 copy-done.1
  7.5 122.8 %shard_map.136.projected = bf16[16,48,2048]{2,1,0:T(8,128)(2,1)} custom-call(s32[16]{0:T(128)} %copy-done.1, s32[16]{0:T(128)} %get-tuple-element.6.slot_of, s32[16]{0:T(128)} %get-tuple-element.5.rank_of, s32[8]{0:T(128)} %bitcast_subtract_fusion.starts, bf16[16,48,2048]{2,1,0:T(8,128)(2,1)} %bitcast.9, f32[1,2048]{1,0:T(1,128)} %bitcast.10, ...), custom_call_target="tpu_custom_call" | custom-call | tf_op jit(solution)/shard_map/pallas_call | solution.py:320
  130.3 3.8 %shard_map.137 = bf16[16,48,2048]{2,1,0:T(8,128)(2,1)} custom-call(s32[16]{0:T(128)} %select_reduce_fusion.rank_for, bf16[16,48,2048]{2,1,0:T(8,128)(2,1)} %shard_map.136.projected), custom_call_target="tpu_custom_call" | custom-call | tf_op jit(solution)/shard_map/pallas_call | solution.py:388
Async XLA Ops:
  0.0 2.0 %copy-start = (s32[16,8]{0,1:T(8,128)S(1)}, s32[16,8]{0,1:T(8,128)}, u32[]{:S(2)}) copy-start(s32[16,8]{0,1:T(8,128)} %param.20) | copy-start | bytes 1540
  3.5 4.0 %copy-start.1 = (s32[16]{0:T(128)}, s32[16]{0:T(128)S(1)}, u32[]{:S(2)}) copy-start(s32[16]{0:T(128)S(1)} %get-tuple-element.7.sent) | copy-start | bytes 196

commit v4 on v3

v4 whole, which is shorter than its diff:
```python
import jax
import jax.numpy as jnp
import numpy as np
from jax import lax
from jax.experimental import pallas as pl
from jax.experimental.pallas import tpu as pltpu
from jax.sharding import PartitionSpec as P

PIECE = 48
SUB = 12
TOGETHER = 4
WIDE = 12
LAST = 2
MESH = pl.DeviceIdType.MESH
rms_epsilon = 1e-06
ORDER = [(0, 1), (0, 3), (1, 0), (3, 0), (1, 1), (3, 3), (1, 3), (3, 1), (0, 2), (2, 0), (1, 2), (2, 3), (3, 2), (2, 1), (2, 2)]
WINDOW = 8
DOWN = sum(step[0] * 4**n for n, step in enumerate(ORDER))
RIGHT = sum(step[1] * 4**n for n, step in enumerate(ORDER))


def decay_sums():
    row = np.arange(PIECE)[:, None]
    col = np.arange(PIECE)[None, :]

    def between(low, high):
        return ((col > low) & (col <= high)).astype(np.float32)

    mid = (row // SUB) * SUB + SUB // 2 - 1
    near = between(mid, row) - between(row, mid)
    half = (row // (2 * SUB)) * (2 * SUB) + SUB - 1
    pair = between(half, row) + between(row, half)
    middle = np.full_like(row, 2 * SUB - 1)
    whole = between(middle, row) + between(row, middle)
    before = between(np.full_like(row, -1), row)[: 2 * SUB]
    after = between(row, np.full_like(row, PIECE - 1))[2 * SUB :]
    sums = np.concatenate([near, pair, whole, before, after], axis=0)
    return np.concatenate([sums, sums], axis=1)


def head_spread(heads, size):
    return np.tile(np.repeat(np.eye(heads, dtype=np.float32), size, axis=1), (3, 1))


def split(x):
    high = x.astype(jnp.bfloat16)
    return high, x - high.astype(jnp.float32)


def dot_nt(a, b):
    return lax.dot_general(a, b, (((1,), (1,)), ((), ())), preferred_element_type=jnp.float32)


def dot_tn(a, b):
    return lax.dot_general(a, b, (((0,), (0,)), ((), ())), preferred_element_type=jnp.float32)


def peer_along(rank, sign):
    me = lax.axis_index("dp")
    at = rank - 1
    power = 1 + 3 * (at % 2)
    power = power * (1 + 15 * (at // 2 % 2))
    power = power * (1 + 255 * (at // 4 % 2))
    power = power * (1 + 65535 * (at // 8))
    row = (me // 4 + 4 + sign * (DOWN // power % 4)) % 4
    column = (me % 4 + 4 + sign * (RIGHT // power % 4)) % 4
    return row * 4 + column


def peers_along(sign):
    me = lax.axis_index("dp")
    return [me] + [
        (me // 4 + 4 + sign * down) % 4 * 4 + (me % 4 + 4 + sign * right) % 4
        for down, right in ORDER
    ]


def layer_kernel(
    source_dp, source_offset, doc_lengths, tokens, gain_ref, weight, beta_ref, bias_ref, sums_ref,
    spread_ref, out_weight, result, rank_for,
    sent, slot_of, rank_of, starts, held, send, recv, weight_held, out_weight_held, normed, qkv, strength_ref, logs, gaps, stepped_ref, mixes,
    out_ref, carry_ref, change_ref, decay_ref, state, total, prefix_ref, totals_ref,
    chain_send, chain_recv, back_send, back_recv, gathered,
    token_sem, weight_sem, out_weight_sem, send_sem, recv_sem,
    chain_send_sem, chain_recv_sem, back_send_sem, back_recv_sem, result_sem,
):
    groups, piece_rows, model_width = held.shape
    heads, size, _ = state.shape
    width = heads * size
    me, seq = lax.axis_index("dp"), lax.axis_index("seq")
    peers = lax.axis_size("seq")
    following, previous = lax.rem(seq + 1, peers), lax.rem(seq + peers - 1, peers)

    def within(index):
        return jnp.clip(index, 0, groups - 1)

    token_copy = pltpu.make_async_copy(tokens, held, token_sem)
    token_copy.start()
    weight_copy = pltpu.make_async_copy(weight, weight_held, weight_sem)
    out_weight_copy = pltpu.make_async_copy(out_weight, out_weight_held, out_weight_sem)
    barrier = pltpu.get_barrier_semaphore()
    for distance in range(1, groups):
        pl.semaphore_signal(
            barrier, inc=1, device_id=(lax.rem(me + distance, groups), seq), device_id_type=MESH
        )
    pl.semaphore_signal(barrier, inc=1, device_id=(me, following), device_id_type=MESH)
    pl.semaphore_signal(barrier, inc=1, device_id=(me, previous), device_id_type=MESH)
    @pl.loop(0, groups)
    def _(target):
        offset = jnp.int32(0)
        for slot in range(groups):
            here = source_dp[target, seq, slot] == me
            offset = offset + jnp.where(here, source_offset[target, seq, slot], 0)
        sent[target] = offset // PIECE

    token_copy.wait()
    weight_copy.start()
    out_weight_copy.start()
    send[0] = held[within(sent[me])]
    own_copy = pltpu.make_async_copy(send.at[0], recv.at[0], recv_sem.at[0])
    own_copy.start()

    @pl.when(seq == 0)
    def _():
        chain_recv[...] = jnp.zeros_like(chain_recv)

    def arriving(rank):
        target = peer_along(rank, 1)
        return pltpu.make_async_remote_copy(
            src_ref=send.at[rank], dst_ref=recv.at[rank], send_sem=send_sem.at[rank],
            recv_sem=recv_sem.at[rank], device_id=(target, seq), device_id_type=MESH,
        )

    def launch(rank):
        send[rank] = held[within(sent[peer_along(rank, 1)])]
        arriving(rank).start()

    pl.semaphore_wait(barrier, groups + 1)
    pl.loop(1, WINDOW)(launch)
    sources = peers_along(-1)
    owners = peers_along(1)

    @pl.loop(0, groups)
    def _(slot):
        source = source_dp[me, seq, slot]
        rank = jnp.int32(0)
        for n in range(1, groups):
            rank = rank + jnp.where(source == sources[n], n, 0)
        rank_of[slot] = rank

    @pl.loop(0, groups)
    def _(rank):
        slot = jnp.int32(0)
        for n in range(1, groups):
            slot = slot + jnp.where(rank_of[n] == rank, n, 0)
        slot_of[rank] = slot

    @pl.loop(0, groups)
    def _(piece):
        rank = jnp.int32(0)
        for n in range(1, groups):
            rank = rank + jnp.where(sent[owners[n]] == piece, n, 0)
        rank_for[piece] = within(rank)

    begin = jnp.int32(0)
    for n in range(starts.shape[0]):
        starts[n] = begin
        begin = begin + doc_lengths[n, me]
    weight_copy.wait()

    down = lax.broadcasted_iota(jnp.int32, (PIECE, PIECE), 0)
    across = lax.broadcasted_iota(jnp.int32, (PIECE, PIECE), 1)
    wide = lax.broadcasted_iota(jnp.int32, (PIECE, size), 0)
    causal = down >= across
    in_sub = causal & (down // SUB == across // SUB)
    in_pair = causal & (down // (2 * SUB) == across // (2 * SUB)) & (down // SUB != across // SUB)
    in_whole = causal & (down // (2 * SUB) != across // (2 * SUB))
    right_pair = (wide // SUB) % 2 == 1

    def document_of(position):
        count = jnp.zeros_like(position)
        for n in range(starts.shape[0]):
            count = count + (starts[n] <= position).astype(jnp.int32)
        return count

    def local_part(inside, rank):
        first = (seq * groups + within(slot_of[rank])) * PIECE
        doc_down = document_of(first + down)
        doc_across = document_of(first + across)
        doc_wide = document_of(first + wide)
        doc_before = document_of(first - 1)
        doc_last = document_of(first + PIECE - 1)
        same = doc_down == doc_across
        near_mask, pair_mask, whole_mask = in_sub & same, in_pair & same, in_whole & same
        reaches = (doc_wide == doc_before).astype(jnp.float32)
        stays = (doc_wide == doc_last).astype(jnp.float32)
        kept = (doc_last == doc_before).astype(jnp.float32)
        head_cols = [slice(h * size, (h + 1) * size) for h in range(heads)]
        squares = []
        for cols in head_cols:
            key = qkv[1, inside, :, cols].astype(jnp.float32)
            high, low = split(key * key)
            squares.append(jnp.concatenate([high, low.astype(jnp.bfloat16)], axis=1))
        norms = jnp.dot(
            jnp.concatenate(squares, axis=0), jnp.ones((2 * size, size), jnp.bfloat16),
            preferred_element_type=jnp.float32,
        )
        for h, cols in enumerate(head_cols):
            key = qkv[1, inside, :, cols].astype(jnp.float32)
            now = strength_ref[inside, :, cols]
            step = now / (1.0 + now * norms[h * PIECE : (h + 1) * PIECE])
            stepped_ref[:, cols] = (qkv[2, inside, :, cols].astype(jnp.float32) * step).astype(
                jnp.bfloat16
            )
            high, low = split(jnp.log2(1.0 - step * (key * key)))
            logs[:PIECE, cols] = high
            logs[PIECE:, cols] = low.astype(jnp.bfloat16)
        for start in range(0, width, 2 * size):
            cols = slice(start, start + 2 * size)
            gaps[:, cols] = jnp.dot(
                sums_ref[...], logs[:, cols], preferred_element_type=jnp.float32
            )
        middle = 2 * SUB
        for h, cols in enumerate(head_cols):
            query = qkv[0, inside, :, cols].astype(jnp.float32)
            key = qkv[1, inside, :, cols].astype(jnp.float32)
            near = gaps[:PIECE, cols]
            mixes[0, :, cols] = (query * jnp.exp2(near)).astype(jnp.bfloat16)
            mixes[1, :, cols] = (key * jnp.exp2(-near)).astype(jnp.bfloat16)
            pair = jnp.exp2(gaps[PIECE : 2 * PIECE, cols])
            mixes[2, :, cols] = (jnp.where(right_pair, query, key) * pair).astype(jnp.bfloat16)
            whole = jnp.exp2(gaps[2 * PIECE : 3 * PIECE, cols])
            mixes[3, :, cols] = (
                jnp.concatenate([key[:middle], query[middle:]], axis=0) * whole
            ).astype(jnp.bfloat16)
            first_half = jnp.exp2(gaps[3 * PIECE : 3 * PIECE + middle, cols])
            second_half = jnp.exp2(gaps[3 * PIECE + middle :, cols])
            before = jnp.concatenate(
                [first_half, whole[middle:] * first_half[middle - 1 :]], axis=0
            )
            after = jnp.concatenate(
                [whole[:middle] * whole[PIECE - 1 :], second_half], axis=0
            )
            carry_ref[rank, :, cols] = (query * (before * reaches)).astype(jnp.bfloat16)
            mixes[4, :, cols] = (key * (after * stays)).astype(jnp.bfloat16)
            decay_ref[rank, h : h + 1, :] = before[PIECE - 1 :, :] * kept
        for h, cols in enumerate(head_cols):
            scores = jnp.where(
                near_mask,
                dot_nt(mixes[0, :, cols], mixes[1, :, cols]),
                jnp.where(
                    pair_mask,
                    dot_nt(mixes[2, :, cols], mixes[2, :, cols]),
                    jnp.where(whole_mask, dot_nt(mixes[3, :, cols], mixes[3, :, cols]), 0.0),
                ),
            )
            out_ref[rank, :, cols] = jnp.dot(
                scores.astype(jnp.bfloat16), stepped_ref[:, cols],
                preferred_element_type=jnp.float32,
            )
            change_ref[rank, h] = dot_tn(stepped_ref[:, cols], mixes[4, :, cols])

    def arrived(first, together):
        for n in range(together):
            rank = first + n
            pltpu.make_async_copy(send.at[rank], recv.at[rank], recv_sem.at[rank]).wait()

            @pl.when(rank + WINDOW < groups)
            def _():
                launch(rank + WINDOW)

            rows = recv[rank].astype(jnp.float32)
            normed[n * PIECE : (n + 1) * PIECE, :] = (
                rows
                * lax.rsqrt(jnp.mean(rows * rows, axis=1, keepdims=True) + rms_epsilon)
                * gain_ref[...]
            ).astype(jnp.bfloat16)
        rows_now = normed[: together * PIECE, :]
        strength = 1.0 / (1.0 + jnp.exp(-(dot_nt(rows_now, beta_ref[...]) + bias_ref[...])))
        high, rest = split(strength)
        middle, rest = split(rest)
        parts = jnp.concatenate([high, middle, rest.astype(jnp.bfloat16)], axis=1)
        for start in range(0, width, 2 * size):
            cols = slice(start, start + 2 * size)
            spread = jnp.dot(parts, spread_ref[:, cols], preferred_element_type=jnp.float32)
            for n in range(together):
                strength_ref[n, :, cols] = spread[n * PIECE : (n + 1) * PIECE]
        tile = 512
        for part in range(3):
            for start in range(0, width, tile):
                cols = slice(start, start + tile)
                product = jnp.dot(
                    rows_now, weight_held[part, :, cols], preferred_element_type=jnp.float32
                ).astype(jnp.bfloat16)
                for n in range(together):
                    qkv[part, n, :, cols] = product[n * PIECE : (n + 1) * PIECE]

        @pl.loop(0, together)
        def _(inside):
            local_part(inside, first + inside)

    @pl.loop(0, WIDE // TOGETHER)
    def _(group):
        arrived(group * TOGETHER, TOGETHER)

    @pl.loop(0, (groups - WIDE) // LAST)
    def _(group):
        arrived(WIDE + group * LAST, LAST)

    state[...] = jnp.zeros_like(state)
    total[...] = jnp.ones_like(total)

    @pl.loop(0, groups)
    def _(slot):
        rank = within(rank_of[slot])
        for h in range(heads):
            prefix_ref[slot, h] = state[h].astype(jnp.bfloat16)
            state[h] = state[h] * decay_ref[rank, h : h + 1, :] + change_ref[rank, h]
        totals_ref[slot] = total[...]
        total[...] = total[...] * decay_ref[rank]

    def add_earlier(rank):
        slot = within(slot_of[rank])
        for h in range(heads):
            cols = slice(h * size, (h + 1) * size)
            carried = carry_ref[rank, :, cols]
            out_ref[rank, :, cols] += dot_nt(carried, prefix_ref[slot, h])
            carry_ref[rank, :, cols] = (
                carried.astype(jnp.float32) * totals_ref[slot, h : h + 1, :]
            ).astype(jnp.bfloat16)

    ahead = 2 * (seq + 1)
    pl.loop(0, ahead)(add_earlier)
    links = [
        pltpu.make_async_remote_copy(
            src_ref=chain_send.at[h], dst_ref=chain_recv.at[h], send_sem=chain_send_sem.at[h],
            recv_sem=chain_recv_sem.at[h], device_id=(me, following), device_id_type=MESH,
        )
        for h in range(heads)
    ]
    for h in range(heads):
        @pl.when(seq > 0)
        def _():
            links[h].wait_recv()

        @pl.when(seq < peers - 1)
        def _():
            before = chain_recv[h].astype(jnp.float32)
            chain_send[h] = (before * total[h : h + 1, :] + state[h]).astype(jnp.bfloat16)
            links[h].start()

    pl.loop(ahead, groups)(add_earlier)

    def finished(rank):
        for h in range(heads):
            cols = slice(h * size, (h + 1) * size)
            yield cols, (
                out_ref[rank, :, cols] + dot_nt(carry_ref[rank, :, cols], chain_recv[h])
            ).astype(jnp.bfloat16)

    def leaving(rank):
        return pltpu.make_async_remote_copy(
            src_ref=back_send.at[rank], dst_ref=back_recv.at[rank],
            send_sem=back_send_sem.at[rank], recv_sem=back_recv_sem.at[rank],
            device_id=(peer_along(rank, -1), seq), device_id_type=MESH,
        )

    @pl.loop(1, groups)
    def _(rank):
        for cols, part in finished(rank):
            back_send[rank, :, cols] = part
        leaving(rank).start()

    for cols, part in finished(0):
        back_send[0, :, cols] = part
    own_back = pltpu.make_async_copy(back_send.at[0], back_recv.at[0], back_recv_sem.at[0])
    own_back.start()
    out_weight_copy.wait()

    @pl.loop(0, groups // TOGETHER)
    def _(group):
        for n in range(TOGETHER):
            rank = group * TOGETHER + n
            pltpu.make_async_copy(
                back_send.at[rank], back_recv.at[rank], back_recv_sem.at[rank]
            ).wait()
            gathered[n * PIECE : (n + 1) * PIECE, :] = back_recv[rank]
        tile = 512
        for start in range(0, model_width, tile):
            cols = slice(start, start + tile)
            product = jnp.dot(
                gathered[...], out_weight_held[:, cols], preferred_element_type=jnp.float32
            ).astype(jnp.bfloat16)
            for n in range(TOGETHER):
                held[group * TOGETHER + n, :, cols] = product[n * PIECE : (n + 1) * PIECE]
        for n in range(TOGETHER):
            rank = group * TOGETHER + n
            pltpu.make_async_copy(held.at[rank], result.at[rank], result_sem.at[rank]).start()

    for rank in range(groups):
        pltpu.make_async_copy(held.at[rank], result.at[rank], result_sem.at[rank]).wait()
    @pl.loop(1, groups)
    def _(rank):
        arriving(rank).wait_send()
        leaving(rank).wait_send()

    @pl.when(seq < peers - 1)
    def _():
        for link in links:
            link.wait_send()


def layer(
    source_dp, source_offset, doc_lengths, tokens, gain, weight, beta, bias, out_weight
):
    groups = source_dp.shape[0]
    rows, model_width = tokens.shape
    width = weight.shape[2]
    heads = beta.shape[1]
    size = width // heads
    smem = pl.BlockSpec(memory_space=pltpu.SMEM)
    vmem = pl.BlockSpec(memory_space=pltpu.VMEM)
    hbm = pl.BlockSpec(memory_space=pl.ANY)
    pieces = (groups, PIECE, model_width)
    narrow = (groups, PIECE, width)
    states = (heads, size, size)
    bfloat16, float32 = jnp.bfloat16, jnp.float32
    sems = pltpu.SemaphoreType.DMA((groups,))
    head_sems = pltpu.SemaphoreType.DMA((heads,))
    sums = jnp.asarray(decay_sums(), bfloat16)
    spread = jnp.asarray(head_spread(heads, size), bfloat16)
    return pl.pallas_call(
        layer_kernel,
        out_shape=(
            jax.ShapeDtypeStruct(pieces, bfloat16),
            jax.ShapeDtypeStruct((groups,), jnp.int32),
        ),
        in_specs=[smem] * 3 + [hbm, vmem, hbm, vmem, vmem, vmem, vmem, hbm],
        out_specs=(hbm, smem),
        scratch_shapes=[
            pltpu.SMEM((groups,), jnp.int32),
            pltpu.SMEM((groups,), jnp.int32),
            pltpu.SMEM((groups,), jnp.int32),
            pltpu.SMEM((doc_lengths.shape[0],), jnp.int32),
            pltpu.VMEM(pieces, bfloat16),
            pltpu.VMEM(pieces, bfloat16),
            pltpu.VMEM(pieces, bfloat16),
            pltpu.VMEM(weight.shape, bfloat16),
            pltpu.VMEM(out_weight.shape, bfloat16),
            pltpu.VMEM((TOGETHER * PIECE, model_width), bfloat16),
            pltpu.VMEM((3, TOGETHER, PIECE, width), bfloat16),
            pltpu.VMEM((TOGETHER, PIECE, width), float32),
            pltpu.VMEM((2 * PIECE, width), bfloat16),
            pltpu.VMEM((4 * PIECE, width), float32),
            pltpu.VMEM((PIECE, width), bfloat16),
            pltpu.VMEM((5, PIECE, width), bfloat16),
            pltpu.VMEM(narrow, float32),
            pltpu.VMEM(narrow, bfloat16),
            pltpu.VMEM((groups,) + states, float32),
            pltpu.VMEM((groups, heads, size), float32),
            pltpu.VMEM(states, float32),
            pltpu.VMEM((heads, size), float32),
            pltpu.VMEM((groups,) + states, bfloat16),
            pltpu.VMEM((groups, heads, size), float32),
            pltpu.VMEM(states, bfloat16),
            pltpu.VMEM(states, bfloat16),
            pltpu.VMEM(narrow, bfloat16),
            pltpu.VMEM(narrow, bfloat16),
            pltpu.VMEM((TOGETHER * PIECE, width), bfloat16),
            pltpu.SemaphoreType.DMA,
            pltpu.SemaphoreType.DMA,
            pltpu.SemaphoreType.DMA,
            sems,
            sems,
            head_sems,
            head_sems,
            sems,
            sems,
            sems,
        ],
        compiler_params=pltpu.CompilerParams(
            collective_id=0, has_side_effects=True, vmem_limit_bytes=60 << 20
        ),
    )(
        source_dp, source_offset, doc_lengths, tokens.reshape(pieces), gain.reshape(1, -1), weight,
        beta.T, bias.reshape(1, -1), sums, spread, out_weight,
    )


def place_kernel(rank_for, projected, result, held, in_sems, out_sems):
    pieces = projected.shape[0]
    arrive = [
        pltpu.make_async_copy(projected.at[jnp.clip(rank_for[n], 0, pieces - 1)], held.at[n], in_sems.at[n])
        for n in range(pieces)
    ]
    leave = [
        pltpu.make_async_copy(held.at[n], result.at[n], out_sems.at[n]) for n in range(pieces)
    ]
    for copy in arrive:
        copy.start()
    for n in range(pieces):
        arrive[n].wait()
        leave[n].start()
    for copy in leave:
        copy.wait()


def place_pieces(rank_for, projected):
    hbm = pl.BlockSpec(memory_space=pl.ANY)
    sems = pltpu.SemaphoreType.DMA((projected.shape[0],))
    return pl.pallas_call(
        place_kernel,
        out_shape=jax.ShapeDtypeStruct(projected.shape, projected.dtype),
        in_specs=[pl.BlockSpec(memory_space=pltpu.SMEM), hbm],
        out_specs=hbm,
        scratch_shapes=[pltpu.VMEM(projected.shape, projected.dtype), sems, sems],
    )(rank_for, projected)


def shards(
    tokens,
    norm_gain,
    qkv_weight,
    beta_weight,
    beta_bias,
    out_weight,
    doc_lengths,
    source_dp,
    source_offset,
):
    projected, rank_for = layer(
        source_dp, source_offset, doc_lengths.T, tokens, norm_gain, qkv_weight, beta_weight,
        beta_bias, out_weight,
    )
    return place_pieces(rank_for, projected).reshape(tokens.shape)


def solution(mesh):
    return jax.shard_map(
        shards,
        mesh=mesh,
        in_specs=(P(("dp", "seq"), None), P(), P(), P(), P(), P(), P(), P(), P()),
        out_specs=P(("dp", "seq"), None),
        check_vma=False,
    )
```

time: 135 us -> 106 us (0.79)
  Pallas kernels: 127 us -> 106 us
  other arithmetic: 4.84 us -> 0 us
  local copies, waits for them, and re-layouts: 2.66 us -> 0 us
    pallas_call x1, Pallas kernels: 123 us -> 102 us  [layer(): pl.pallas_call(layer_kernel, out_shape=(jax.ShapeDtypeStruct(pieces, bflo...]
    reduce_sum x4 -> x0, other arithmetic: 2.8 us -> none  [the longest x1 1.25 us: shards(): sent = jnp.sum(jnp.where(from_here, plan_offset, 0), axis=1) // piece_rows]
    unnamed x5 -> x0, local copies, waits for them, and re-layouts: 1.77 us -> none
where the time goes in v4:
time: 106 us
  Pallas kernels  106 us (100%)
    pallas_call x1, Pallas kernels, layer(): pl.pallas_call(layer_kernel, out_shape=(jax.ShapeDtypeStruct(pieces, bflo...  102 us
    pallas_call x1, Pallas kernels, place_pieces(): pl.pallas_call(place_kernel, out_shape=jax.ShapeDtypeStruct(projected.sha...  3.85 us

profile of v4, /device:TPU:24, one launch (start us, length us, event | category | flops | bytes accessed | tf_op | source)
XLA Modules:
  0.0 105.6 jit_solution(10797907063400532790)
XLA Ops:
  0.0 101.8 %shard_map.109 = (bf16[16,48,2048]{2,1,0:T(8,128)(2,1)}, s32[16]{0:T(128)}) custom-call(s32[16,8,16]{2,1,0:T(8,128)} %source_dp.1, s32[16,8,16]{2,1,0:T(8,128)} %source_offset.1, s32[8,16]{1,0:T(8,128)} %bitcast.9, bf16[16,48,2048]{2,1,0:T(8,128)(2,1)} %bitcast.6, f32[1,2048]{1,0:T(1,128)} %bitcast.8, bf16[3,2048,1024]{2,1,0:T(8,128)(2,1)} %weight.1, ...), custom_call_target="tpu_custom_call" | custom-call | tf_op jit(solution)/shard_map/pallas_call | solution.py:432
  101.8 3.8 %shard_map.110 = bf16[16,48,2048]{2,1,0:T(8,128)(2,1)} custom-call(s32[16]{0:T(128)} %get-tuple-element.7.rank_for, bf16[16,48,2048]{2,1,0:T(8,128)(2,1)} %get-tuple-element.8.projected), custom_call_target="tpu_custom_call" | custom-call | tf_op jit(solution)/shard_map/pallas_call | solution.py:511

commit v5 on v4

--- a/solution.py
+++ b/solution.py
@@ -38,10 +38,6 @@
     return np.concatenate([sums, sums], axis=1)
 
 
-def head_spread(heads, size):
-    return np.tile(np.repeat(np.eye(heads, dtype=np.float32), size, axis=1), (3, 1))
-
-
 def split(x):
     high = x.astype(jnp.bfloat16)
     return high, x - high.astype(jnp.float32)
@@ -77,19 +73,21 @@
 
 def layer_kernel(
     source_dp, source_offset, doc_lengths, tokens, gain_ref, weight, beta_ref, bias_ref, sums_ref,
-    spread_ref, out_weight, result, rank_for,
+    out_weight, result, rank_for,
     sent, slot_of, rank_of, starts, held, send, recv, weight_held, out_weight_held, normed, qkv, strength_ref, logs, gaps, stepped_ref, mixes,
     out_ref, carry_ref, change_ref, decay_ref, state, total, prefix_ref, totals_ref,
-    chain_send, chain_recv, back_send, back_recv, gathered,
+    chain_send, chain_recv, chain_used, pair_recv, pair_total, back_send, back_recv, gathered,
     token_sem, weight_sem, out_weight_sem, send_sem, recv_sem,
-    chain_send_sem, chain_recv_sem, back_send_sem, back_recv_sem, result_sem,
+    pair_sems, chip_sems, relay_sems, total_sems, back_send_sem, back_recv_sem, result_sem,
 ):
     groups, piece_rows, model_width = held.shape
     heads, size, _ = state.shape
     width = heads * size
     me, seq = lax.axis_index("dp"), lax.axis_index("seq")
     peers = lax.axis_size("seq")
-    following, previous = lax.rem(seq + 1, peers), lax.rem(seq + peers - 1, peers)
+    core, chip, chips = seq % 2, seq // 2, peers // 2
+    partner = seq + 1 - 2 * core
+    following, previous = (seq + 2) % peers, (seq + peers - 2) % peers
 
     def within(index):
         return jnp.clip(index, 0, groups - 1)
@@ -105,6 +103,7 @@
         )
     pl.semaphore_signal(barrier, inc=1, device_id=(me, following), device_id_type=MESH)
     pl.semaphore_signal(barrier, inc=1, device_id=(me, previous), device_id_type=MESH)
+    pl.semaphore_signal(barrier, inc=1, device_id=(me, partner), device_id_type=MESH)
     @pl.loop(0, groups)
     def _(target):
         offset = jnp.int32(0)
@@ -120,7 +119,7 @@
     own_copy = pltpu.make_async_copy(send.at[0], recv.at[0], recv_sem.at[0])
     own_copy.start()
 
-    @pl.when(seq == 0)
+    @pl.when(chip == 0)
     def _():
         chain_recv[...] = jnp.zeros_like(chain_recv)
 
@@ -135,7 +134,7 @@
         send[rank] = held[within(sent[peer_along(rank, 1)])]
         arriving(rank).start()
 
-    pl.semaphore_wait(barrier, groups + 1)
+    pl.semaphore_wait(barrier, groups + 2)
     pl.loop(1, WINDOW)(launch)
     sources = peers_along(-1)
     owners = peers_along(1)
@@ -207,7 +206,7 @@
         )
         for h, cols in enumerate(head_cols):
             key = qkv[1, inside, :, cols].astype(jnp.float32)
-            now = strength_ref[inside, :, cols]
+            now = strength_ref[inside, :, h : h + 1]
             step = now / (1.0 + now * norms[h * PIECE : (h + 1) * PIECE])
             stepped_ref[:, cols] = (qkv[2, inside, :, cols].astype(jnp.float32) * step).astype(
                 jnp.bfloat16
@@ -244,7 +243,8 @@
             carry_ref[rank, :, cols] = (query * (before * reaches)).astype(jnp.bfloat16)
             mixes[4, :, cols] = (key * (after * stays)).astype(jnp.bfloat16)
             decay_ref[rank, h : h + 1, :] = before[PIECE - 1 :, :] * kept
-        for h, cols in enumerate(head_cols):
+        weights = []
+        for cols in head_cols:
             scores = jnp.where(
                 near_mask,
                 dot_nt(mixes[0, :, cols], mixes[1, :, cols]),
@@ -254,11 +254,13 @@
                     jnp.where(whole_mask, dot_nt(mixes[3, :, cols], mixes[3, :, cols]), 0.0),
                 ),
             )
+            weights.append(scores.astype(jnp.bfloat16))
+        for h, cols in enumerate(head_cols):
+            change_ref[rank, h] = dot_tn(stepped_ref[:, cols], mixes[4, :, cols])
+        for h, cols in enumerate(head_cols):
             out_ref[rank, :, cols] = jnp.dot(
-                scores.astype(jnp.bfloat16), stepped_ref[:, cols],
-                preferred_element_type=jnp.float32,
+                weights[h], stepped_ref[:, cols], preferred_element_type=jnp.float32
             )
-            change_ref[rank, h] = dot_tn(stepped_ref[:, cols], mixes[4, :, cols])
 
     def arrived(first, together):
         for n in range(together):
@@ -277,14 +279,8 @@
             ).astype(jnp.bfloat16)
         rows_now = normed[: together * PIECE, :]
         strength = 1.0 / (1.0 + jnp.exp(-(dot_nt(rows_now, beta_ref[...]) + bias_ref[...])))
-        high, rest = split(strength)
-        middle, rest = split(rest)
-        parts = jnp.concatenate([high, middle, rest.astype(jnp.bfloat16)], axis=1)
-        for start in range(0, width, 2 * size):
-            cols = slice(start, start + 2 * size)
-            spread = jnp.dot(parts, spread_ref[:, cols], preferred_element_type=jnp.float32)
-            for n in range(together):
-                strength_ref[n, :, cols] = spread[n * PIECE : (n + 1) * PIECE]
+        for n in range(together):
+            strength_ref[n] = strength[n * PIECE : (n + 1) * PIECE]
         tile = 512
         for part in range(3):
             for start in range(0, width, tile):
@@ -321,42 +317,94 @@
 
     def add_earlier(rank):
         slot = within(slot_of[rank])
+        head_cols = [slice(h * size, (h + 1) * size) for h in range(heads)]
+        carried = [carry_ref[rank, :, cols] for cols in head_cols]
+        added = [
+            out_ref[rank, :, cols] + dot_nt(carried[h], prefix_ref[slot, h])
+            for h, cols in enumerate(head_cols)
+        ]
+        for h, cols in enumerate(head_cols):
+            out_ref[rank, :, cols] = added[h]
+            carry_ref[rank, :, cols] = (
+                carried[h].astype(jnp.float32) * totals_ref[slot, h : h + 1, :]
+            ).astype(jnp.bfloat16)
+
+    def link(source, target, h, sems, peer):
+        return pltpu.make_async_remote_copy(
+            src_ref=source.at[h], dst_ref=target.at[h], send_sem=sems.at[0, h],
+            recv_sem=sems.at[1, h], device_id=(me, peer), device_id_type=MESH,
+        )
+
+    def pair_link(h):
+        return link(chain_send, pair_recv, h, pair_sems, partner)
+
+    def chip_link(h):
+        return link(chain_send, chain_recv, h, chip_sems, following)
+
+    def relay_link(h):
+        return link(chain_recv, chain_recv, h, relay_sems, partner)
+
+    decay_link = pltpu.make_async_remote_copy(
+        src_ref=total, dst_ref=pair_total, send_sem=total_sems.at[0], recv_sem=total_sems.at[1],
+        device_id=(me, partner), device_id_type=MESH,
+    )
+
+    @pl.when(core == 0)
+    def _():
+        decay_link.start()
         for h in range(heads):
-            cols = slice(h * size, (h + 1) * size)
-            carried = carry_ref[rank, :, cols]
-            out_ref[rank, :, cols] += dot_nt(carried, prefix_ref[slot, h])
-            carry_ref[rank, :, cols] = (
-                carried.astype(jnp.float32) * totals_ref[slot, h : h + 1, :]
+            chain_send[h] = state[h].astype(jnp.bfloat16)
+            pair_link(h).start()
+
+    pl.loop(0, groups)(add_earlier)
+
+    @pl.when(core == 1)
+    def _():
+        decay_link.wait_recv()
+        for h in range(heads):
+            own_total = total[h : h + 1, :]
+            both_total = own_total * pair_total[h : h + 1, :]
+            pair_link(h).wait_recv()
+            both_state = pair_recv[h].astype(jnp.float32) * own_total + state[h]
+
+            @pl.when(chip > 0)
+            def _():
+                chip_link(h).wait_recv()
+
+            @pl.when(chip < chips - 1)
+            def _():
+                before = chain_recv[h].astype(jnp.float32)
+                chain_send[h] = (before * both_total + both_state).astype(jnp.bfloat16)
+                chip_link(h).start()
+
+            @pl.when(chip > 0)
+            def _():
+                relay_link(h).start()
+
+        for h in range(heads):
+            chain_used[h] = (
+                chain_recv[h].astype(jnp.float32) * pair_total[h : h + 1, :]
+                + pair_recv[h].astype(jnp.float32)
             ).astype(jnp.bfloat16)
 
-    ahead = 2 * (seq + 1)
-    pl.loop(0, ahead)(add_earlier)
-    links = [
-        pltpu.make_async_remote_copy(
-            src_ref=chain_send.at[h], dst_ref=chain_recv.at[h], send_sem=chain_send_sem.at[h],
-            recv_sem=chain_recv_sem.at[h], device_id=(me, following), device_id_type=MESH,
-        )
-        for h in range(heads)
-    ]
-    for h in range(heads):
-        @pl.when(seq > 0)
-        def _():
-            links[h].wait_recv()
-
-        @pl.when(seq < peers - 1)
-        def _():
-            before = chain_recv[h].astype(jnp.float32)
-            chain_send[h] = (before * total[h : h + 1, :] + state[h]).astype(jnp.bfloat16)
-            links[h].start()
-
-    pl.loop(ahead, groups)(add_earlier)
-
-    def finished(rank):
+    @pl.when(core == 0)
+    def _():
         for h in range(heads):
-            cols = slice(h * size, (h + 1) * size)
-            yield cols, (
-                out_ref[rank, :, cols] + dot_nt(carry_ref[rank, :, cols], chain_recv[h])
-            ).astype(jnp.bfloat16)
+            @pl.when(chip > 0)
+            def _():
+                relay_link(h).wait_recv()
+
+            chain_used[h] = chain_recv[h]
+
+
+    def finish(rank):
+        head_cols = [slice(h * size, (h + 1) * size) for h in range(heads)]
+        parts = [
+            out_ref[rank, :, cols] + dot_nt(carry_ref[rank, :, cols], chain_used[h])
+            for h, cols in enumerate(head_cols)
+        ]
+        for h, cols in enumerate(head_cols):
+            back_send[rank, :, cols] = parts[h].astype(jnp.bfloat16)
 
     def leaving(rank):
         return pltpu.make_async_remote_copy(
@@ -367,12 +415,10 @@
 
     @pl.loop(1, groups)
     def _(rank):
-        for cols, part in finished(rank):
-            back_send[rank, :, cols] = part
+        finish(rank)
         leaving(rank).start()
 
-    for cols, part in finished(0):
-        back_send[0, :, cols] = part
+    finish(0)
     own_back = pltpu.make_async_copy(back_send.at[0], back_recv.at[0], back_recv_sem.at[0])
     own_back.start()
     out_weight_copy.wait()
@@ -404,10 +450,22 @@
         arriving(rank).wait_send()
         leaving(rank).wait_send()
 
-    @pl.when(seq < peers - 1)
+    @pl.when(core == 0)
     def _():
-        for link in links:
-            link.wait_send()
+        decay_link.wait_send()
+        for h in range(heads):
+            pair_link(h).wait_send()
+
+    @pl.when(core == 1)
+    def _():
+        for h in range(heads):
+            @pl.when(chip < chips - 1)
+            def _():
+                chip_link(h).wait_send()
+
+            @pl.when(chip > 0)
+            def _():
+                relay_link(h).wait_send()
 
 
 def layer(
@@ -426,16 +484,15 @@
     states = (heads, size, size)
     bfloat16, float32 = jnp.bfloat16, jnp.float32
     sems = pltpu.SemaphoreType.DMA((groups,))
-    head_sems = pltpu.SemaphoreType.DMA((heads,))
+    head_sems = pltpu.SemaphoreType.DMA((2, heads))
     sums = jnp.asarray(decay_sums(), bfloat16)
-    spread = jnp.asarray(head_spread(heads, size), bfloat16)
     return pl.pallas_call(
         layer_kernel,
         out_shape=(
             jax.ShapeDtypeStruct(pieces, bfloat16),
             jax.ShapeDtypeStruct((groups,), jnp.int32),
         ),
-        in_specs=[smem] * 3 + [hbm, vmem, hbm, vmem, vmem, vmem, vmem, hbm],
+        in_specs=[smem] * 3 + [hbm, vmem, hbm, vmem, vmem, vmem, hbm],
         out_specs=(hbm, smem),
         scratch_shapes=[
             pltpu.SMEM((groups,), jnp.int32),
@@ -449,7 +506,7 @@
             pltpu.VMEM(out_weight.shape, bfloat16),
             pltpu.VMEM((TOGETHER * PIECE, model_width), bfloat16),
             pltpu.VMEM((3, TOGETHER, PIECE, width), bfloat16),
-            pltpu.VMEM((TOGETHER, PIECE, width), float32),
+            pltpu.VMEM((TOGETHER, PIECE, heads), float32),
             pltpu.VMEM((2 * PIECE, width), bfloat16),
             pltpu.VMEM((4 * PIECE, width), float32),
             pltpu.VMEM((PIECE, width), bfloat16),
@@ -464,6 +521,9 @@
             pltpu.VMEM((groups, heads, size), float32),
             pltpu.VMEM(states, bfloat16),
             pltpu.VMEM(states, bfloat16),
+            pltpu.VMEM(states, bfloat16),
+            pltpu.VMEM(states, bfloat16),
+            pltpu.VMEM((heads, size), float32),
             pltpu.VMEM(narrow, bfloat16),
             pltpu.VMEM(narrow, bfloat16),
             pltpu.VMEM((TOGETHER * PIECE, width), bfloat16),
@@ -474,6 +534,8 @@
             sems,
             head_sems,
             head_sems,
+            head_sems,
+            pltpu.SemaphoreType.DMA((2,)),
             sems,
             sems,
             sems,
@@ -483,7 +545,7 @@
         ),
     )(
         source_dp, source_offset, doc_lengths, tokens.reshape(pieces), gain.reshape(1, -1), weight,
-        beta.T, bias.reshape(1, -1), sums, spread, out_weight,
+        beta.T, bias.reshape(1, -1), sums, out_weight,
     )
 
 

time: 106 us -> 97.2 us (0.917)
  Pallas kernels: 106 us -> 97 us
    pallas_call x1, Pallas kernels: 102 us -> 93.1 us  [layer(): pl.pallas_call(layer_kernel, out_shape=(jax.ShapeDtypeStruct(pieces, bflo...]
where the time goes in v5:
time: 97.2 us; the launch traced here: 97 us
  Pallas kernels  97 us (100%)
    pallas_call x1, Pallas kernels, layer(): pl.pallas_call(layer_kernel, out_shape=(jax.ShapeDtypeStruct(pieces, bflo...  93.1 us
    pallas_call x1, Pallas kernels, place_pieces(): pl.pallas_call(place_kernel, out_shape=jax.ShapeDtypeStruct(projected.sha...  3.85 us

profile of v5, /device:TPU:24, one launch (start us, length us, event | category | flops | bytes accessed | tf_op | source)
XLA Modules:
  0.0 97.0 jit_solution(11203814875109964192)
XLA Ops:
  0.0 93.1 %shard_map.100 = (bf16[16,48,2048]{2,1,0:T(8,128)(2,1)}, s32[16]{0:T(128)}) custom-call(s32[16,8,16]{2,1,0:T(8,128)} %source_dp.1, s32[16,8,16]{2,1,0:T(8,128)} %source_offset.1, s32[8,16]{1,0:T(8,128)} %bitcast.9, bf16[16,48,2048]{2,1,0:T(8,128)(2,1)} %bitcast.6, f32[1,2048]{1,0:T(1,128)} %bitcast.8, bf16[3,2048,1024]{2,1,0:T(8,128)(2,1)} %weight.1, ...), custom_call_target="tpu_custom_call" | custom-call | tf_op jit(solution)/shard_map/pallas_call | solution.py:489
  93.1 3.8 %shard_map.101 = bf16[16,48,2048]{2,1,0:T(8,128)(2,1)} custom-call(s32[16]{0:T(128)} %get-tuple-element.7.rank_for, bf16[16,48,2048]{2,1,0:T(8,128)(2,1)} %get-tuple-element.8.projected), custom_call_target="tpu_custom_call" | custom-call | tf_op jit(solution)/shard_map/pallas_call | solution.py:573

commit v6 on v5

--- a/solution.py
+++ b/solution.py
@@ -130,12 +130,20 @@
             recv_sem=recv_sem.at[rank], device_id=(target, seq), device_id_type=MESH,
         )
 
+    def stage(rank):
+        send[rank] = held[within(sent[peer_along(rank, 1)])]
+
     def launch(rank):
-        send[rank] = held[within(sent[peer_along(rank, 1)])]
+        stage(rank)
         arriving(rank).start()
 
+    pl.loop(1, WINDOW)(stage)
     pl.semaphore_wait(barrier, groups + 2)
-    pl.loop(1, WINDOW)(launch)
+
+    @pl.loop(1, WINDOW)
+    def _(rank):
+        arriving(rank).start()
+
     sources = peers_along(-1)
     owners = peers_along(1)
 

time: 97.2 us -> 97.2 us (level)
  no operation moved by 1% of the time
where the time goes in v6:
time: 97.2 us; the launch traced here: 96.9 us
  Pallas kernels  96.9 us (100%)
    pallas_call x1, Pallas kernels, layer(): pl.pallas_call(layer_kernel, out_shape=(jax.ShapeDtypeStruct(pieces, bflo...  93.1 us
    pallas_call x1, Pallas kernels, place_pieces(): pl.pallas_call(place_kernel, out_shape=jax.ShapeDtypeStruct(projected.sha...  3.85 us

profile of v6, /device:TPU:24, one launch (start us, length us, event | category | flops | bytes accessed | tf_op | source)
XLA Modules:
  0.0 96.9 jit_solution(17795387359064844424)
XLA Ops:
  0.0 93.1 %shard_map.100 = (bf16[16,48,2048]{2,1,0:T(8,128)(2,1)}, s32[16]{0:T(128)}) custom-call(s32[16,8,16]{2,1,0:T(8,128)} %source_dp.1, s32[16,8,16]{2,1,0:T(8,128)} %source_offset.1, s32[8,16]{1,0:T(8,128)} %bitcast.9, bf16[16,48,2048]{2,1,0:T(8,128)(2,1)} %bitcast.6, f32[1,2048]{1,0:T(1,128)} %bitcast.8, bf16[3,2048,1024]{2,1,0:T(8,128)(2,1)} %weight.1, ...), custom_call_target="tpu_custom_call" | custom-call | tf_op jit(solution)/shard_map/pallas_call | solution.py:497
  93.1 3.8 %shard_map.101 = bf16[16,48,2048]{2,1,0:T(8,128)(2,1)} custom-call(s32[16]{0:T(128)} %get-tuple-element.7.rank_for, bf16[16,48,2048]{2,1,0:T(8,128)(2,1)} %get-tuple-element.8.projected), custom_call_target="tpu_custom_call" | custom-call | tf_op jit(solution)/shard_map/pallas_call | solution.py:581
